TPU v7x, 32 devices: a whole 2x2x4 slice. The times are simulated.
32 devices in a mesh: dp: 8 (over y, x, core), blk: 4 (over z).
Axes of the slice: x: 2, y: 2, z: 4, core: 2. Of those that a mesh axis runs over, the one named last changes fastest.
Arguments:
- speech: bfloat16 [16, 864, 768], P('dp', 'blk'), may hold values from -6 to 6
- lengths: int32 [16], P('dp'), may hold values from 144 to 864, as said below
- grad_output: bfloat16 [16, 864, 768], P('dp', 'blk'), may hold values from -6 to 6
- w_qkv: bfloat16 [768, 2304], replicated, may hold values from -0.3125 to 0.3125
- bias_query: float32 [768], replicated, may hold values from -2 to 2
- bias_value: float32 [768], replicated, may hold values from -2 to 2
- w_out: bfloat16 [768, 768], replicated, may hold values from -0.875 to 0.875
- bias_out: float32 [768], replicated, may hold values from -2 to 2
- gain_first: float32 [768], replicated, may hold values from 0.1 to 1.9
- shift_first: float32 [768], replicated, may hold values from -2 to 2
- w_up: bfloat16 [768, 3072], replicated, may hold values from -0.21875 to 0.21875
- bias_up: float32 [3072], replicated, may hold values from -2 to 2
- w_down: bfloat16 [3072, 768], replicated, may hold values from -0.109375 to 0.109375
- bias_down: float32 [768], replicated, may hold values from -2 to 2
- gain_second: float32 [768], replicated, may hold values from 0.1 to 1.9
- shift_second: float32 [768], replicated, may hold values from -2 to 2
Outputs:
- output: bfloat16 [16, 864, 768], P('dp', 'blk')
- grad_speech: float32 [16, 864, 768], P('dp', 'blk')
- grad_w_qkv: float32 [768, 2304], P('dp', 'blk')
- grad_bias_query: float32 [768], replicated
- grad_bias_value: float32 [768], replicated
- grad_w_out: float32 [768, 768], P('dp', 'blk')
- grad_bias_out: float32 [768], replicated
- grad_gain_first: float32 [768], replicated
- grad_shift_first: float32 [768], replicated
- grad_w_up: float32 [768, 3072], P('dp', 'blk')
- grad_bias_up: float32 [3072], replicated
- grad_w_down: float32 [3072, 768], P('dp', 'blk')
- grad_bias_down: float32 [768], replicated
- grad_gain_second: float32 [768], replicated
- grad_shift_second: float32 [768], replicated
Inputs may be any that keep to these rules, and one draw needn't show every extreme that they name: `lengths`: in each group of 2 utterances held by one index of dp, one has all 864 frames.
All inputs are finite; a program needn't handle non-finite values.
Results may differ from a plain program's by a relative error of at most 0.019.
Values may be sent and summed in bfloat16 or wider, within the bound.
A program may use at most 192 MiB of HBM per device.

v0:
```python
import jax
import jax.numpy as jnp
from jax import lax
from jax.sharding import PartitionSpec as P

H = 12


norm_epsilon = 1e-05
masked_score = -1000000000.0


def shifted(block, axis, distance):
    devices = range(lax.axis_size(axis))
    route = [((i - distance) % len(devices), i) for i in devices]
    return lax.ppermute(block, axis, route)


def norm_forward(values, gain_vec, shift_vec):
    average = jnp.mean(values, axis=-1, keepdims=True)
    centered = values - average
    inverse = lax.rsqrt(jnp.mean(centered * centered, axis=-1, keepdims=True) + norm_epsilon)
    normal = centered * inverse
    return (normal * gain_vec + shift_vec, normal, inverse)


def norm_backward(upstream, normal, inverse, gain_vec):
    scaled = upstream * gain_vec
    grad_in = inverse * (
        scaled
        - jnp.mean(scaled, axis=-1, keepdims=True)
        - normal * jnp.mean(scaled * normal, axis=-1, keepdims=True)
    )
    return (grad_in, jnp.sum(upstream * normal, axis=0), jnp.sum(upstream, axis=0))


def sum_over_utterances(mats):
    return (
        lax.psum_scatter(mats[0], "dp", scatter_dimension=0, tiled=True),
        lax.psum_scatter(mats[1], "dp", scatter_dimension=0, tiled=True),
        lax.psum_scatter(mats[2], "dp", scatter_dimension=0, tiled=True),
        lax.psum_scatter(mats[3], "dp", scatter_dimension=0, tiled=True),
    )


def sum_over_blocks(mats):
    return (
        lax.psum_scatter(
            mats[0].astype(jnp.bfloat16), "blk", scatter_dimension=1, tiled=True
        ).astype(jnp.float32),
        lax.psum_scatter(
            mats[1].astype(jnp.bfloat16), "blk", scatter_dimension=1, tiled=True
        ).astype(jnp.float32),
        lax.psum_scatter(
            mats[2].astype(jnp.bfloat16), "blk", scatter_dimension=1, tiled=True
        ).astype(jnp.float32),
        lax.psum_scatter(
            mats[3].astype(jnp.bfloat16), "blk", scatter_dimension=1, tiled=True
        ).astype(jnp.float32),
    )


def shards(
    speech,
    lengths,
    grad_output,
    w_qkv,
    bias_query,
    bias_value,
    w_out,
    bias_out,
    gain_first,
    shift_first,
    w_up,
    bias_up,
    w_down,
    bias_down,
    gain_second,
    shift_second,
):
    utterances, block_len, model_width = speech.shape
    head_count = H
    head_size = model_width // head_count
    score_scale = head_size ** (-0.5)
    cycle_size = lax.axis_size("blk")
    own_index = lax.axis_index("blk")
    token_rows = speech.reshape(utterances * block_len, model_width)

    def split_heads(block):
        return block.reshape(block.shape[0], block.shape[1], head_count, head_size)

    no_bias = jnp.zeros_like(bias_query)
    projected = jnp.dot(token_rows, w_qkv, preferred_element_type=jnp.float32)
    projected = projected + jnp.concatenate([bias_query, no_bias, bias_value])
    projected = projected.astype(jnp.bfloat16).reshape(utterances, block_len, 3, model_width)
    queries = projected[:, :, 0]
    key_rows = projected[:, :, 1]
    value_rows = projected[:, :, 2]
    query_heads = split_heads(queries)

    def block_scores(key_block, first_key):
        positions = first_key + jnp.arange(key_block.shape[1], dtype=jnp.int32)
        usable = positions[None, :] < lengths[:, None]
        scores = (
            jnp.einsum(
                "uqhd,ukhd->uhqk",
                query_heads,
                split_heads(key_block),
                preferred_element_type=jnp.float32,
            )
            * score_scale
        )
        return (scores, usable[:, None, None, :])

    stacked_kv = jnp.stack([key_rows, value_rows])
    softmax_state = (
        jnp.full((utterances, head_count, block_len), -1e30, jnp.float32),
        jnp.zeros((utterances, head_count, block_len), jnp.float32),
        jnp.zeros((utterances, head_count, block_len, head_size), jnp.float32),
    )
    moving = stacked_kv
    for rotation in range(cycle_size):
        source = (own_index - rotation) % cycle_size
        absorb_running_max, absorb_total_weight, absorb_weighted = softmax_state
        absorb_scores, absorb_usable = block_scores(moving[0], source * block_len)
        absorb_scores = jnp.where(absorb_usable, absorb_scores, masked_score)
        new_max = jnp.maximum(absorb_running_max, jnp.max(absorb_scores, axis=-1))
        rescale = jnp.exp(absorb_running_max - new_max)
        weights = jnp.where(absorb_usable, jnp.exp(absorb_scores - new_max[..., None]), 0.0)
        absorb_total_weight = absorb_total_weight * rescale + jnp.sum(weights, axis=-1)
        absorb_weighted = absorb_weighted * rescale[..., None] + jnp.einsum(
            "uhqk,ukhd->uhqd",
            weights.astype(jnp.bfloat16),
            split_heads(moving[1]),
            preferred_element_type=jnp.float32,
        )
        softmax_state = (new_max, absorb_total_weight, absorb_weighted)
        if rotation + 1 < cycle_size:
            moving = shifted(moving, "blk", 1)
    running_max, total_weight, weighted = softmax_state
    attended = weighted / total_weight[..., None]
    log_total = running_max + jnp.log(total_weight)
    attended_low = attended.transpose(0, 2, 1, 3).reshape(utterances * block_len, model_width)
    attended_low = attended_low.astype(jnp.bfloat16)
    attn_out = jnp.dot(attended_low, w_out, preferred_element_type=jnp.float32) + bias_out
    hidden = token_rows.astype(jnp.float32) + attn_out
    normed, normal_first, inverse_first = norm_forward(hidden, gain_first, shift_first)
    normed_low = normed.astype(jnp.bfloat16)
    upward = jnp.dot(normed_low, w_up, preferred_element_type=jnp.float32) + bias_up
    active_low = jax.nn.gelu(upward, approximate=False).astype(jnp.bfloat16)
    branch = jnp.dot(active_low, w_down, preferred_element_type=jnp.float32) + bias_down
    result, normal_second, inverse_second = norm_forward(normed + branch, gain_second, shift_second)
    output = result.reshape(utterances, block_len, model_width).astype(jnp.bfloat16)
    grad_rows = grad_output.reshape(utterances * block_len, model_width).astype(jnp.float32)
    grad_sum2, grad_gain_second, grad_shift_second = norm_backward(
        grad_rows, normal_second, inverse_second, gain_second
    )
    grad_branch = grad_sum2.astype(jnp.bfloat16)
    grad_bias_down = jnp.sum(grad_branch.astype(jnp.float32), axis=0)
    grad_w_down = jnp.dot(active_low.T, grad_branch, preferred_element_type=jnp.float32)
    grad_active = jnp.dot(grad_branch, w_down.T, preferred_element_type=jnp.float32)
    normal_cdf = 0.5 * (1.0 + lax.erf(upward * 0.7071067811865476))
    density = jnp.exp(-0.5 * upward * upward) * 0.3989422804014327
    grad_upward = (grad_active * (normal_cdf + upward * density)).astype(jnp.bfloat16)
    grad_bias_up = jnp.sum(grad_upward.astype(jnp.float32), axis=0)
    grad_w_up = jnp.dot(normed_low.T, grad_upward, preferred_element_type=jnp.float32)
    grad_normed = grad_sum2 + jnp.dot(grad_upward, w_up.T, preferred_element_type=jnp.float32)
    grad_hidden, grad_gain_first, grad_shift_first = norm_backward(
        grad_normed, normal_first, inverse_first, gain_first
    )
    grad_attn = grad_hidden.astype(jnp.bfloat16)
    grad_bias_out = jnp.sum(grad_attn.astype(jnp.float32), axis=0)
    grad_w_out = jnp.dot(attended_low.T, grad_attn, preferred_element_type=jnp.float32)
    grad_attended = jnp.dot(grad_attn, w_out.T, preferred_element_type=jnp.float32).astype(
        jnp.bfloat16
    )
    grad_heads = grad_attended.reshape(utterances, block_len, head_count, head_size)
    row_dot = jnp.sum(grad_heads.transpose(0, 2, 1, 3).astype(jnp.float32) * attended, axis=-1)
    moving = stacked_kv
    carried = jnp.zeros((2, utterances, block_len, model_width), jnp.float32)
    grad_query = jnp.zeros((utterances, block_len, head_count, head_size), jnp.float32)
    for rotation in range(cycle_size):
        source = (own_index - rotation) % cycle_size
        release_key_block = moving[0]
        release_scores, release_usable = block_scores(release_key_block, source * block_len)
        probabilities = jnp.where(
            release_usable, jnp.exp(release_scores - log_total[..., None]), 0.0
        )
        grad_probs = jnp.einsum(
            "uqhd,ukhd->uhqk",
            grad_heads,
            split_heads(moving[1]),
            preferred_element_type=jnp.float32,
        )
        grad_scores = (probabilities * (grad_probs - row_dot[..., None])).astype(jnp.bfloat16)
        part_query = (
            jnp.einsum(
                "uhqk,ukhd->uqhd",
                grad_scores,
                split_heads(release_key_block),
                preferred_element_type=jnp.float32,
            )
            * score_scale
        )
        part_keys = (
            jnp.einsum(
                "uhqk,uqhd->ukhd", grad_scores, query_heads, preferred_element_type=jnp.float32
            )
            * score_scale
        )
        part_values = jnp.einsum(
            "uhqk,uqhd->ukhd",
            probabilities.astype(jnp.bfloat16),
            grad_heads,
            preferred_element_type=jnp.float32,
        )
        key_count = release_key_block.shape[1]
        part_query, part_keys, part_values = (
            part_query,
            part_keys.reshape(utterances, key_count, model_width),
            part_values.reshape(utterances, key_count, model_width),
        )
        grad_query = grad_query + part_query
        carried = carried + jnp.stack([part_keys, part_values])
        if rotation + 1 < cycle_size:
            moving = shifted(moving, "blk", 1)
        carried = shifted(carried.astype(jnp.bfloat16), "blk", 1).astype(carried.dtype)
    query_grad_low = grad_query.reshape(utterances * block_len, model_width).astype(jnp.bfloat16)
    keys_grad_low = carried[0].reshape(utterances * block_len, model_width).astype(jnp.bfloat16)
    values_grad_low = carried[1].reshape(utterances * block_len, model_width).astype(jnp.bfloat16)
    grad_projected = jnp.concatenate([query_grad_low, keys_grad_low, values_grad_low], axis=1)
    grad_bias_query = jnp.sum(grad_projected[:, :model_width].astype(jnp.float32), axis=0)
    grad_bias_value = jnp.sum(grad_projected[:, 2 * model_width :].astype(jnp.float32), axis=0)
    grad_w_qkv = jnp.dot(token_rows.T, grad_projected, preferred_element_type=jnp.float32)
    grad_speech = grad_hidden + jnp.dot(grad_projected, w_qkv.T, preferred_element_type=jnp.float32)
    grad_speech = grad_speech.reshape(utterances, block_len, model_width)
    vectors = lax.psum(
        (
            grad_bias_query,
            grad_bias_value,
            grad_bias_out,
            grad_gain_first,
            grad_shift_first,
            grad_bias_up,
            grad_bias_down,
            grad_gain_second,
            grad_shift_second,
        ),
        ("dp", "blk"),
    )
    matrices = (grad_w_qkv, grad_w_out, grad_w_up, grad_w_down)
    summed = sum_over_blocks(sum_over_utterances(matrices))
    return (
        output,
        grad_speech,
        summed[0],
        vectors[0],
        vectors[1],
        summed[1],
        vectors[2],
        vectors[3],
        vectors[4],
        summed[2],
        vectors[5],
        summed[3],
        vectors[6],
        vectors[7],
        vectors[8],
    )


def solution(mesh):
    return jax.shard_map(
        shards,
        mesh=mesh,
        in_specs=(
            P("dp", "blk", None),
            P("dp"),
            P("dp", "blk", None),
            P(),
            P(),
            P(),
            P(),
            P(),
            P(),
            P(),
            P(),
            P(),
            P(),
            P(),
            P(),
            P(),
        ),
        out_specs=(
            P("dp", "blk", None),
            P("dp", "blk", None),
            P("dp", "blk"),
            P(),
            P(),
            P("dp", "blk"),
            P(),
            P(),
            P(),
            P("dp", "blk"),
            P(),
            P("dp", "blk"),
            P(),
            P(),
            P(),
        ),
        check_vma=False,
    )
```

profile of v0, /device:TPU:0, one launch (start us, length us, event | category | flops | bytes accessed | tf_op | source)
XLA Modules:
  0.0 570.8 jit_solution(14231721702403146860)
XLA Ops:
  9.2 4.1 fusion.16
  13.3 6.5 %reshape.310 = bf16[2,216,3,768]{3,2,1,0:T(4,128)(2,1)} reshape(bf16[432,2304]{1,0:T(8,128)(2,1)} %fusion.16) | data formatting | bytes 3981312 | tf_op jit(solution)/shard_map/reshape | solution.py:95
  19.8 7.0 %fusion.126 = (bf16[2,216,1,768]{3,2,1,0:T(2,128)(2,1)}, bf16[2,216,1,768]{3,2,1,0:T(2,128)(2,1)S(1)}, bf16[2,216,1,768]{3,2,1,0:T(2,128)(2,1)S(1)}) fusion(bf16[2,216,3,768]{3,2,1,0:T(4,128)(2,1)} %reshape.310), kind=kLoop, calls=%fused_computation.218 | loop fusion | bytes 3981312 | tf_op jit(solution)/shard_map/slice | solution.py:96
  31.8 3.7 copy.171
  35.4 3.7 copy.170
  41.8 3.7 copy.169
  48.5 5.6 select_reduce_fusion.3
  54.1 9.2 %collective-permute-done = bf16[2,2,216,768]{3,2,1,0:T(8,128)(2,1)} collective-permute-done((bf16[2,2,216,768]{3,2,1,0:T(8,128)(2,1)}, bf16[2,2,216,768]{3,2,1,0:T(8,128)(2,1)}, u32[]{:S(2)}, u32[]{:S(2)}) %collective-permute-start) | collective-permute-done | bytes 1327136 | tf_op jit(solution)/shard_map/ppermute | solution.py:16
  68.0 5.6 select_reduce_fusion.2
  77.2 4.7 fusion.23
  81.9 3.7 fusion.56
  85.7 14.7 %collective-permute-done.1 = bf16[2,2,216,768]{3,2,1,0:T(8,128)(2,1)} collective-permute-done((bf16[2,2,216,768]{3,2,1,0:T(8,128)(2,1)}, bf16[2,2,216,768]{3,2,1,0:T(8,128)(2,1)}, u32[]{:S(2)}, u32[]{:S(2)}) %collective-permute-start.1) | collective-permute-done | bytes 1327136 | tf_op jit(solution)/shard_map/ppermute | solution.py:16
  112.1 5.7 select_reduce_fusion.1
  117.8 14.3 %collective-permute-done.2 = bf16[2,2,216,768]{3,2,1,0:T(8,128)(2,1)} collective-permute-done((bf16[2,2,216,768]{3,2,1,0:T(8,128)(2,1)}, bf16[2,2,216,768]{3,2,1,0:T(8,128)(2,1)}, u32[]{:S(2)}, u32[]{:S(2)}) %collective-permute-start.2) | collective-permute-done | bytes 1327136 | tf_op jit(solution)/shard_map/ppermute | solution.py:16
  152.5 11.7 %convert_element_type.172 = bf16[432,768]{0,1:T(8,128)(2,1)} reshape(bf16[2,216,12,64]{1,0,3,2:T(2,128)(2,1)} %copy.182) | data formatting | bytes 1327104 | tf_op jit(solution)/shard_map/convert_element_type | solution.py:144
  167.4 15.9 %fusion.2 = (bf16[432,3072]{1,0:T(8,128)(2,1)S(1)}, f32[432,3072]{1,0:T(8,128)S(1)}) fusion(f32[3072]{0:T(1024)S(1)} %copy-done.68, bf16[768,3072]{1,0:T(8,128)(2,1)} %param.26, f32[432,768]{1,0:T(8,128)S(1)} %get-tuple-element.138, f32[768]{0:T(1024)S(1)} %copy-done.70, f32[768]{0:T(1024)S(1)} %copy-done.67, f32[432]{0:T(512)S(1)} %add_rsqrt_fusion.1, ...), kind=kOutput, calls=%fused_computation.5 | convolution fusion | flops 2127679488 | bytes 14030208 | tf_op jit(solution)/shard_map/dot_general | solution.py:149
  189.2 4.6 convert_reduce_fusion
  201.4 8.5 %fusion.95 = f32[3072,768]{1,0:T(8,128)} fusion(bf16[432,3072]{1,0:T(8,128)(2,1)} %copy-done.71, f32[432,768]{1,0:T(8,128)} %copy-done.34), kind=kOutput, calls=%fused_computation.191 | convolution fusion | flops 2038763520 | bytes 13418496 | tf_op jit(solution)/shard_map/dot_general | solution.py:160
  210.6 8.8 %fusion.119 = f32[768,3072]{1,0:T(8,128)} fusion(bf16[432,3072]{1,0:T(8,128)(2,1)} %copy-done.72, f32[432,768]{1,0:T(8,128)} %copy-done.29, f32[768]{0:T(1024)} %param.25, f32[768]{0:T(1024)} %param.24, f32[432]{0:T(512)} %copy-done.65, f32[432]{0:T(512)S(1)} %copy-done.58), kind=kOutput, calls=%fused_computation.215 | convolution fusion | flops 2040090624 | bytes 13428096 | tf_op jit(solution)/shard_map/dot_general | solution.py:166
  219.6 3.6 convolution_convert_fusion
  223.2 3.3 reshape.320
  231.0 4.8 fusion.75
  238.2 4.4 fusion.68
  242.6 4.5 multiply_convert_fusion.3
  253.9 6.0 %fusion.33 = f32[2,12,64,216]{3,2,1,0:T(8,128)} fusion(bf16[2,216,12,64]{1,3,2,0:T(8,128)(2,1)S(1)} %copy-done.9, f32[2,12,216,216]{2,3,1,0:T(8,128)} %get-tuple-element.132, f32[2,12,216]{2,1,0:T(8,128)S(1)} %copy-done.41, pred[2,216]{1,0:T(4,128)(4,1)S(1)} %get-tuple-element.124), kind=kOutput, calls=%fused_computation.60 | convolution fusion | flops 147806208 | bytes 6490800 | tf_op jit(solution)/shard_map/uhqk,uqhd->ukhd/dot_general | solution.py:211
  259.9 3.3 copy.207
  263.2 5.0 multiply_convert_fusion.2
  270.4 3.3 copy.206
  273.7 10.5 %collective-permute-done.3 = bf16[2,2,216,768]{3,2,1,0:T(8,128)(2,1)} collective-permute-done((bf16[2,2,216,768]{3,2,1,0:T(8,128)(2,1)}, bf16[2,2,216,768]{3,2,1,0:T(8,128)(2,1)}, u32[]{:S(2)}, u32[]{:S(2)}) %collective-permute-start.3) | collective-permute-done | bytes 1327136 | tf_op jit(solution)/shard_map/ppermute | solution.py:16
  284.2 3.7 fusion.37
  288.1 4.9 fusion.31
  296.0 5.1 multiply_convert_fusion.1
  306.2 11.3 %collective-permute-done.4 = bf16[2,2,216,768]{3,2,1,0:T(8,128)(2,1)} collective-permute-done((bf16[2,2,216,768]{3,2,1,0:T(8,128)(2,1)}, bf16[2,2,216,768]{3,2,1,0:T(8,128)(2,1)}, u32[]{:S(2)}, u32[]{:S(2)}) %collective-permute-start.4) | collective-permute-done | bytes 1327136 | tf_op jit(solution)/shard_map/ppermute | solution.py:16
  317.5 3.6 fusion.38
  321.1 5.0 fusion.29
  329.1 5.7 %multiply_convert_fusion = bf16[2,12,216,216]{2,3,1,0:T(8,128)(2,1)S(1)} fusion(f32[2,12,216,216]{2,3,1,0:T(8,128)} %copy-done.6, f32[2,12,216]{2,1,0:T(8,128)} %copy-done.56, f32[2,12,216]{2,1,0:T(8,128)} %copy-done.39, pred[2,216]{1,0:T(4,128)(4,1)S(1)} %get-tuple-element.125, bf16[2,216,12,64]{1,3,2,0:T(8,128)(2,1)} %copy.184, ...), kind=kOutput, calls=%fused_computation.13 | convolution fusion | flops 150045696 | bytes 8087472 | tf_op jit(solution)/shard_map/uqhd,ukhd->uhqk/dot_general | solution.py:189
  337.3 3.3 copy.216
  340.5 9.0 %collective-permute-done.5 = bf16[2,2,216,768]{3,2,1,0:T(8,128)(2,1)} collective-permute-done((bf16[2,2,216,768]{3,2,1,0:T(8,128)(2,1)}, bf16[2,2,216,768]{3,2,1,0:T(8,128)(2,1)}, u32[]{:S(2)}, u32[]{:S(2)}) %collective-permute-start.5) | collective-permute-done | bytes 1327136 | tf_op jit(solution)/shard_map/ppermute | solution.py:16
  349.6 3.5 fusion.39
  361.5 3.3 convert_element_type.191
  364.8 16.0 %collective-permute-done.6 = bf16[2,2,216,768]{3,2,1,0:T(8,128)(2,1)} collective-permute-done((bf16[2,2,216,768]{3,2,1,0:T(8,128)(2,1)}, bf16[2,2,216,768]{3,2,1,0:T(8,128)(2,1)}, u32[]{:S(2)}, u32[]{:S(2)}) %collective-permute-start.6) | collective-permute-done | bytes 1327136 | tf_op jit(solution)/shard_map/ppermute | solution.py:16
  388.0 6.6 %convolution_bitcast_fusion = f32[768,2304]{0,1:T(8,128)} fusion(bf16[432,768]{1,0:T(8,128)(2,1)} %bitcast.259, bf16[432,768]{0,1:T(8,128)(2,1)} %copy.219, bf16[432,768]{0,1:T(8,128)(2,1)} %copy.218, bf16[432,768]{0,1:T(8,128)(2,1)} %convert_element_type.191), kind=kOutput, calls=%fused_computation.2 | convolution fusion | flops 1534795776 | bytes 9732096 | tf_op jit(solution)/shard_map/dot_general | solution.py:234
  394.7 8.1 %copy.242 = f32[768,2304]{1,0:T(8,128)} copy(f32[768,2304]{0,1:T(8,128)} %convolution_bitcast_fusion) | data formatting | bytes 14155776
  413.4 58.4 %reduce-scatter.25.cloned.1.call-done = f32[96,2304]{1,0:T(8,128)} async-done(((f32[768,2304]{1,0:T(8,128)}), f32[96,2304]{1,0:T(8,128)}) %reduce-scatter.25.cloned.1.call-update) | async-done | bytes 884752
  474.7 19.1 %reduce-scatter.27.cloned.1.call-done = bf16[192,96]{1,0:T(8,128)(2,1)} async-done(((bf16[768,96]{1,0:T(8,128)(2,1)}), bf16[192,96]{1,0:T(8,128)(2,1)}) %reduce-scatter.27.cloned.1.call-update) | async-done | bytes 36880
  498.0 40.3 %all-reduce = (f32[768]{0:T(1024)}, f32[768]{0:T(1024)}, f32[768]{0:T(1024)}, f32[768]{0:T(1024)}, f32[768]{0:T(1024)}, /*index=5*/f32[3072]{0:T(1024)}, f32[768]{0:T(1024)}, f32[768]{0:T(1024)}, f32[768]{0:T(1024)}) all-reduce(f32[768]{0:T(1024)} %reduce_sum.226, ...), channel_id=1, replica_groups=mesh['dp'=8,'blk'=4] {'dp','blk'}, use_global_device_ids=true, to_apply=%region_20.21 | all-reduce | flops 9216 | bytes 73728 | tf_op jit(solution)/shard_map/psum | solution.py:237
  538.3 5.2 convolution_add_fusion.2
  548.7 13.1 %reduce-scatter.15.cloned.1.call-done = bf16[96,576]{0,1:T(8,128)(2,1)} async-done(((bf16[96,2304]{0,1:T(8,128)(2,1)}), bf16[96,576]{0,1:T(8,128)(2,1)}) %reduce-scatter.15.cloned.1.call-update) | async-done | bytes 110608 | tf_op jit(solution)/shard_map/reduce_scatter | solution.py:48
  (270 shorter events, 139.8 us)
Async XLA Ops:
  7.2 395.7 %reduce-scatter.17.cloned.1.call-start = ((), (), s32[]{:S(2)}) async-start(), calls=%async_computation.9 | async-start | bytes 2654208 | tf_op jit(solution)/shard_map/reduce_scatter | solution.py:40
  28.7 10.4 %copy-start.55 = (f32[768]{0:T(1024)S(1)}, f32[768]{0:T(1024)}, u32[]{:S(2)}) copy-start(f32[768]{0:T(1024)} %param.30) | copy-start | bytes 9220
  28.7 34.5 %collective-permute-start = (bf16[2,2,216,768]{3,2,1,0:T(8,128)(2,1)}, bf16[2,2,216,768]{3,2,1,0:T(8,128)(2,1)}, u32[]{:S(2)}, u32[]{:S(2)}) collective-permute-start(bf16[2,2,216,768]{3,2,1,0:T(8,128)(2,1)} %pad_maximum_fusion.1), channel_id=1, source_target_pairs={{3,0},{0,1},{1,2},{2,3},{7,4},{4,5},{5,6},{6,7},{11,8},{8,9},{9,10... | collective-permute-start | bytes 3981320 | tf_op jit(solution)/shard_map/ppermute | solution.py:16
  46.2 7.8 %copy-start.59 = (pred[2,216]{1,0:T(4,128)(4,1)}, pred[2,216]{1,0:T(4,128)(4,1)S(1)}, u32[]{:S(2)}) copy-start(pred[2,216]{1,0:T(4,128)(4,1)S(1)} %get-tuple-element.126) | copy-start | bytes 1300
  67.9 32.4 %collective-permute-start.1 = (bf16[2,2,216,768]{3,2,1,0:T(8,128)(2,1)}, bf16[2,2,216,768]{3,2,1,0:T(8,128)(2,1)}, u32[]{:S(2)}, u32[]{:S(2)}) collective-permute-start(bf16[2,2,216,768]{3,2,1,0:T(8,128)(2,1)} %collective-permute-done), channel_id=1, source_target_pairs={{3,0},{0,1},{1,2},{2,3},{7,4},{4,5},{5,6},{6,7},{11,8},{8,9},{9,10... | collective-permute-start | bytes 3981320 | tf_op jit(solution)/shard_map/ppermute | solution.py:16
  77.2 4.7 copy-start.44
  77.2 4.7 copy-start.5
  81.9 18.7 %slice-start = ((s8[5308416]{0:T(1024)(128)(4,1)}), s8[4194304]{0:T(1024)(128)(4,1)S(1)}, s32[]{:S(2)}) async-start(s8[5308416]{0:T(1024)(128)(4,1)} %bitcast.220), calls=%async_computation.16 | async-start | bytes 8388608
  81.9 18.7 %slice-start.1 = ((s8[5308416]{0:T(1024)(128)(4,1)}), s8[1114112]{0:T(1024)(128)(4,1)S(1)}, s32[]{:S(2)}) async-start(s8[5308416]{0:T(1024)(128)(4,1)} %bitcast.220), calls=%async_computation.17 | async-start | bytes 2228224
  81.9 18.7 %copy-start.60 = (pred[2,216]{1,0:T(4,128)(4,1)S(1)}, pred[2,216]{1,0:T(4,128)(4,1)}, u32[]{:S(2)}) copy-start(pred[2,216]{1,0:T(4,128)(4,1)} %copy-done.59) | copy-start | bytes 1300
  100.4 31.7 %collective-permute-start.2 = (bf16[2,2,216,768]{3,2,1,0:T(8,128)(2,1)}, bf16[2,2,216,768]{3,2,1,0:T(8,128)(2,1)}, u32[]{:S(2)}, u32[]{:S(2)}) collective-permute-start(bf16[2,2,216,768]{3,2,1,0:T(8,128)(2,1)} %collective-permute-done.1), channel_id=1, source_target_pairs={{3,0},{0,1},{1,2},{2,3},{7,4},{4,5},{5,6},{6,7},{11,8},{8,9},{9,10... | collective-permute-start | bytes 3981320 | tf_op jit(solution)/shard_map/ppermute | solution.py:16
  142.0 5.7 copy-start.6
  142.1 5.6 copy-start.47
  164.3 19.0 %slice-start.2 = ((s8[4718592]{0:T(1024)(128)(4,1)}), s8[4194304]{0:T(1024)(128)(4,1)S(1)}, s32[]{:S(2)}) async-start(s8[4718592]{0:T(1024)(128)(4,1)} %bitcast.253), calls=%async_computation.18 | async-start | bytes 8388608
  167.0 30.0 %copy-start.29 = (f32[432,768]{1,0:T(8,128)}, f32[432,768]{1,0:T(8,128)S(1)}, u32[]{:S(2)}) copy-start(f32[432,768]{1,0:T(8,128)S(1)} %get-tuple-element.138) | copy-start | bytes 3981316
  167.0 30.0 %copy-start.57 = (f32[432]{0:T(512)}, f32[432]{0:T(512)S(1)}, u32[]{:S(2)}) copy-start(f32[432]{0:T(512)S(1)} %broadcast_multiply_fusion.5) | copy-start | bytes 5188
  167.4 29.7 %copy-start.65 = (f32[432]{0:T(512)}, f32[432]{0:T(512)S(1)}, u32[]{:S(2)}) copy-start(f32[432]{0:T(512)S(1)} %add_rsqrt_fusion.1) | copy-start | bytes 5188
  167.4 15.9 %slice-start.3 = ((s8[4718592]{0:T(1024)(128)(4,1)}), s8[524288]{0:T(1024)(128)(4,1)S(1)}, s32[]{:S(2)}) async-start(s8[4718592]{0:T(1024)(128)(4,1)} %bitcast.253), calls=%async_computation.19 | async-start | bytes 1048576
  167.4 15.9 %copy-start.69 = (f32[768]{0:T(1024)S(1)}, f32[768]{0:T(1024)}, u32[]{:S(2)}) copy-start(f32[768]{0:T(1024)} %param.29) | copy-start | bytes 9220
  187.2 6.6 %slice-start.4 = ((s8[4718592]{0:T(1024)(128)(4,1)}), s8[4194304]{0:T(1024)(128)(4,1)S(1)}, s32[]{:S(2)}) async-start(s8[4718592]{0:T(1024)(128)(4,1)} %bitcast.255), calls=%async_computation.20 | async-start | bytes 8388608
  189.2 4.6 copy-start.34
  189.2 4.6 slice-start.5
  201.3 205.0 %reduce-scatter.23.cloned.1.call-start = ((), (), s32[]{:S(2)}) async-start(), calls=%async_computation.12 | async-start | bytes 10616832 | tf_op jit(solution)/shard_map/reduce_scatter | solution.py:42
  209.9 200.9 %reduce-scatter.19.cloned.1.call-start = ((), (), s32[]{:S(2)}) async-start(), calls=%async_computation.10 | async-start | bytes 10616832 | tf_op jit(solution)/shard_map/reduce_scatter | solution.py:41
  219.4 252.4 %reduce-scatter.25.cloned.1.call-start = ((), (), s32[]{:S(2)}) async-start(), calls=%async_computation.13 | async-start | bytes 7962624
  223.2 7.8 %copy-start.61 = (pred[2,216]{1,0:T(4,128)(4,1)S(1)}, pred[2,216]{1,0:T(4,128)(4,1)}, u32[]{:S(2)}) copy-start(pred[2,216]{1,0:T(4,128)(4,1)} %copy-done.59) | copy-start | bytes 1300
  231.0 4.8 copy-start.39
  242.6 4.5 copy-start.56
  242.6 4.5 copy-start.1
  253.9 30.3 %collective-permute-start.3 = (bf16[2,2,216,768]{3,2,1,0:T(8,128)(2,1)}, bf16[2,2,216,768]{3,2,1,0:T(8,128)(2,1)}, u32[]{:S(2)}, u32[]{:S(2)}) collective-permute-start(bf16[2,2,216,768]{3,2,1,0:T(8,128)(2,1)} %pad_maximum_fusion.2), channel_id=1, source_target_pairs={{3,0},{0,1},{1,2},{2,3},{7,4},{4,5},{5,6},{6,7},{11,8},{8,9},{9,10... | collective-permute-start | bytes 3981320 | tf_op jit(solution)/shard_map/ppermute | solution.py:16
  263.2 5.0 copy-start.2
  273.7 14.4 %copy-start.10 = (bf16[2,216,12,64]{1,3,2,0:T(8,128)(2,1)S(1)}, bf16[2,216,12,64]{1,3,2,0:T(8,128)(2,1)}, u32[]{:S(2)}) copy-start(bf16[2,216,12,64]{1,3,2,0:T(8,128)(2,1)} %copy.184) | copy-start | bytes 1990660
  273.7 14.4 %copy-start.42 = (f32[2,12,216]{2,1,0:T(8,128)S(1)}, f32[2,12,216]{2,1,0:T(8,128)}, u32[]{:S(2)}) copy-start(f32[2,12,216]{2,1,0:T(8,128)} %copy-done.39) | copy-start | bytes 62212
  287.9 29.6 %collective-permute-start.4 = (bf16[2,2,216,768]{3,2,1,0:T(8,128)(2,1)}, bf16[2,2,216,768]{3,2,1,0:T(8,128)(2,1)}, u32[]{:S(2)}, u32[]{:S(2)}) collective-permute-start(bf16[2,2,216,768]{3,2,1,0:T(8,128)(2,1)} %fusion.37), channel_id=1, source_target_pairs={{3,0},{0,1},{1,2},{2,3},{7,4},{4,5},{5,6},{6,7},{11,8},{8,9},{9,10... | collective-permute-start | bytes 3981320 | tf_op jit(solution)/shard_map/ppermute | solution.py:16
  296.0 5.1 copy-start.3
  306.2 14.9 %copy-start.11 = (bf16[2,216,12,64]{1,3,2,0:T(8,128)(2,1)S(1)}, bf16[2,216,12,64]{1,3,2,0:T(8,128)(2,1)}, u32[]{:S(2)}) copy-start(bf16[2,216,12,64]{1,3,2,0:T(8,128)(2,1)} %copy.184) | copy-start | bytes 1990660
  306.2 14.9 %copy-start.43 = (f32[2,12,216]{2,1,0:T(8,128)S(1)}, f32[2,12,216]{2,1,0:T(8,128)}, u32[]{:S(2)}) copy-start(f32[2,12,216]{2,1,0:T(8,128)} %copy-done.39) | copy-start | bytes 62212
  321.1 28.4 %collective-permute-start.5 = (bf16[2,2,216,768]{3,2,1,0:T(8,128)(2,1)}, bf16[2,2,216,768]{3,2,1,0:T(8,128)(2,1)}, u32[]{:S(2)}, u32[]{:S(2)}) collective-permute-start(bf16[2,2,216,768]{3,2,1,0:T(8,128)(2,1)} %fusion.38), channel_id=1, source_target_pairs={{3,0},{0,1},{1,2},{2,3},{7,4},{4,5},{5,6},{6,7},{11,8},{8,9},{9,10... | collective-permute-start | bytes 3981320 | tf_op jit(solution)/shard_map/ppermute | solution.py:16
  329.1 5.8 %copy-start.4 = (bf16[2,216,1,768]{1,3,0,2:T(8,128)(2,1)S(1)}, bf16[2,216,1,768]{1,3,0,2:T(8,128)(2,1)}, u32[]{:S(2)}) copy-start(bf16[2,216,1,768]{1,3,0,2:T(8,128)(2,1)} %copy.169) | copy-start | bytes 1990660
  340.5 12.8 %copy-start.18 = (bf16[2,12,216,216]{2,3,1,0:T(8,128)(2,1)S(1)}, bf16[2,12,216,216]{2,3,1,0:T(8,128)(2,1)}, u32[]{:S(2)}) copy-start(bf16[2,12,216,216]{2,3,1,0:T(8,128)(2,1)} %copy-done.17) | copy-start | bytes 6718468
  340.5 12.8 %copy-start.24 = (bf16[2,216,1,768]{1,3,0,2:T(8,128)(2,1)S(1)}, bf16[2,216,1,768]{1,3,0,2:T(8,128)(2,1)}, u32[]{:S(2)}) copy-start(bf16[2,216,1,768]{1,3,0,2:T(8,128)(2,1)} %copy.170) | copy-start | bytes 1990660
  353.1 27.8 %collective-permute-start.6 = (bf16[2,2,216,768]{3,2,1,0:T(8,128)(2,1)}, bf16[2,2,216,768]{3,2,1,0:T(8,128)(2,1)}, u32[]{:S(2)}, u32[]{:S(2)}) collective-permute-start(bf16[2,2,216,768]{3,2,1,0:T(8,128)(2,1)} %fusion.39), channel_id=1, source_target_pairs={{3,0},{0,1},{1,2},{2,3},{7,4},{4,5},{5,6},{6,7},{11,8},{8,9},{9,10... | collective-permute-start | bytes 3981320 | tf_op jit(solution)/shard_map/ppermute | solution.py:16
  402.8 91.0 %reduce-scatter.27.cloned.1.call-start = ((), (), s32[]{:S(2)}) async-start(), calls=%async_computation.14 | async-start | bytes 245760
  406.3 137.3 %reduce-scatter.29.cloned.1.call-start = ((), (), s32[]{:S(2)}) async-start(), calls=%async_computation.15 | async-start | bytes 737280
  410.7 87.3 %copy-start.62 = (f32[768]{0:T(1024)S(1)}, f32[768]{0:T(1024)}, u32[]{:S(2)}) copy-start(f32[768]{0:T(1024)} %get-tuple-element.81) | copy-start | bytes 9220
  410.7 87.3 %copy-start.63 = (f32[768]{0:T(1024)S(1)}, f32[768]{0:T(1024)}, u32[]{:S(2)}) copy-start(f32[768]{0:T(1024)} %get-tuple-element.78) | copy-start | bytes 9220
  410.7 136.3 %reduce-scatter.21.cloned.1.call-start = ((), (), s32[]{:S(2)}) async-start(), calls=%async_computation.11 | async-start | bytes 737280 | tf_op jit(solution)/shard_map/reduce_scatter | solution.py:54
  413.4 148.4 %reduce-scatter.15.cloned.1.call-start = ((), (), s32[]{:S(2)}) async-start(), calls=%async_computation.8 | async-start | bytes 737280 | tf_op jit(solution)/shard_map/reduce_scatter | solution.py:48
  (46 other events, 105.5 us)
Sparse Core Ops, SparseCore 0:
  201.4 40.1 reduce-scatter.16
  245.6 76.4 reduce-scatter.22
  326.0 76.4 reduce-scatter.18
  406.3 65.4 reduce-scatter.24
  474.5 19.3 reduce-scatter.26
  496.1 20.3 reduce-scatter.28
  518.9 20.0 reduce-scatter.20
  541.4 20.3 reduce-scatter.14
where the time goes:
time: 582 us; the launch traced here: 571 us
  waiting for transfers between devices  176 us (30%)
  matrix products  150 us (26%)
  local copies, waits for them, and re-layouts  132 us (23%)
  other arithmetic  53.1 us (9%)
  blocking collectives  40.3 us (7%)
  between operations  15.5 us (3%)
    ppermute x7, waiting for transfers between devices, shifted(): return lax.ppermute(block, axis, route)  85.1 us
    unnamed x11, waiting for transfers between devices  77.6 us
    psum x1, blocking collectives, shards(): lax.psum((grad_bias_query, grad_bias_value, grad_bias_out, grad_gain_firs...  40.3 us
    unnamed x167, local copies, waits for them, and re-layouts  30 us
    another operation x8, local copies, waits for them, and re-layouts, shards(): carried = carried + jnp.stack([part_keys, part_values])  23.2 us
    dot_general x4, matrix products, shards(): jnp.einsum('uhqk,uqhd->ukhd', probabilities.astype(jnp.bfloat16), grad_he...  20.8 us
    dot_general x4, matrix products, shards(): jnp.einsum('uqhd,ukhd->uhqk', grad_heads, split_heads(moving[1]), preferr...  20.4 us
    dot_general x4, matrix products, block_scores(): jnp.einsum('uqhd,ukhd->uhqk', query_heads, split_heads(key_block), prefer...  19.7 us
  transfers between devices with their start and end apart: 15, of which 10 were waited for; matrix products, arithmetic and copies ran while one was open for 41% of the time, Pallas kernels for 0%

commit v1 on v0

v1 whole, which is shorter than its diff:
```python
import functools

import jax
import jax.numpy as jnp
from jax import lax
from jax.experimental import pallas as pl
from jax.experimental.pallas import tpu as pltpu
from jax.sharding import PartitionSpec as P

MESH = pl.DeviceIdType.MESH
VMEM = pltpu.VMEM
F32, BF16 = jnp.float32, jnp.bfloat16
H = 12
EPS = 1e-05
MASKED = -1000000000.0
NN = (((1,), (0,)), ((), ()))
NT = (((1,), (1,)), ((), ()))
ANY = pl.BlockSpec(memory_space=pl.ANY)
VM = pl.BlockSpec(memory_space=pltpu.VMEM)


def dot(a, b, dims=NN):
    return lax.dot_general(a, b, dims, preferred_element_type=F32)


def low(v):
    return v.astype(BF16)


def split3(v):
    hi = low(v)
    rest = v - hi.astype(F32)
    mid = low(rest)
    return hi.astype(F32), mid.astype(F32), rest - mid.astype(F32)


def place():
    dp = lax.axis_index("dp")
    return dp, lax.axis_index("blk"), lax.rem(dp, 2)


def lane_of(shape):
    return lax.broadcasted_iota(jnp.int32, shape, len(shape) - 1)


def attend_kernel(geo, x_ref, g_ref, lens_ref, w_hbm, b_ref,
                  xm, gm, qa, kall, vall, kb, o_ref,
                  w_ref, lens, q_scr, wsem, sx, rx, sg, rg, skv, rkv, sl):
    nb, hp, blk_len, d = geo
    dp, z, c = place()
    base = dp - c
    peer = (base + 1 - c, z)
    pairs = d // 128
    rows = nb * hp
    wcopy = pltpu.make_async_copy(w_hbm, w_ref, wsem)
    wcopy.start()

    barrier = pltpu.get_barrier_semaphore()
    for dz in range(nb):
        for dc in range(2):
            if dz or dc:
                pl.semaphore_signal(barrier, inc=1, device_id=(base + lax.rem(c + dc, 2), lax.rem(z + dz, nb)),
                                    device_id_type=MESH)
    pl.semaphore_wait(barrier, 2 * nb - 1)

    lens[c] = lens_ref[...]
    lcopy = pltpu.make_async_remote_copy(src_ref=lens_ref, dst_ref=lens.at[c], send_sem=sl.at[0], recv_sem=sl.at[1],
                                         device_id=peer, device_id_type=MESH)
    lcopy.start()

    def pieces(src, dst, ss, rs, start):
        for s in range(2):
            for h in range(2):
                to = 2 * c + s
                here = jnp.logical_and(to == z, c == h)
                part = src.at[s, pl.ds(h * hp, hp)]
                remote = pltpu.make_async_remote_copy(
                    src_ref=part, dst_ref=dst.at[z], send_sem=ss.at[2 * s + h], recv_sem=rs.at[z],
                    device_id=(base + h, to), device_id_type=MESH)

                @pl.when(jnp.logical_not(here))
                def _():
                    remote.start() if start else remote.wait_send()

                if start:
                    @pl.when(here)
                    def _():
                        pltpu.make_async_copy(part, dst.at[z], rs.at[z]).start()

    def arrive(src, dst, rs):
        for i in range(nb):
            pltpu.make_async_copy(src.at[0, pl.ds(0, hp)], dst.at[i], rs.at[i]).wait()

    pieces(x_ref, xm, sx, rx, True)
    wcopy.wait()
    arrive(x_ref, xm, rx)
    pieces(g_ref, gm, sg, rg, True)

    x = xm[...].reshape(rows, d)
    for part, scr in ((1, kall), (2, vall)):
        for p in range(pairs // 2):
            at = part * d + 256 * p
            t = low(dot(x, w_ref[:, at:at + 256]) + b_ref[:, at:at + 256])
            for e in range(2):
                scr[2 * p + e, c] = t[:, 128 * e:128 * e + 128]
    kvs = []
    for n, scr in enumerate((kall, vall)):
        kv = pltpu.make_async_remote_copy(src_ref=scr.at[:, c], dst_ref=scr.at[:, c], send_sem=skv.at[n],
                                          recv_sem=rkv.at[n], device_id=peer, device_id_type=MESH)
        kv.start()
        kvs.append(kv)
    for p in range(pairs // 2):
        at = 256 * p
        t = low(low(dot(x, w_ref[:, at:at + 256]) + b_ref[:, at:at + 256]).astype(F32) * 0.125)
        for e in range(2):
            q_scr[2 * p + e] = t[:, 128 * e:128 * e + 128]

    lcopy.wait()
    usable_len = lens[pl.ds(lax.div(z, 2), 1), pl.ds(lax.rem(z, 2), 1)].reshape(8, 128)[0:1]
    for h in range(2):
        for b in range(nb):
            t = lax.broadcasted_iota(jnp.int32, (hp, 128), 0) + h * hp
            frame = (t + blk_len * b).astype(F32)
            ok = jnp.logical_and(t < blk_len, frame < usable_len)
            kb[pl.ds((h * nb + b) * hp, hp), :] = low(jnp.where(ok, 0.0, MASKED))
    for kv in kvs:
        kv.wait()

    lane1 = lane_of((1, 128))
    lane_q = lane_of((rows, 128))

    def pair_step(p, _):
        kp = kall[p].reshape(2 * rows, 128)
        vp = vall[p].reshape(2 * rows, 128)
        qp = q_scr[p]
        bias = kb[...]
        outs = []
        for e in range(2):
            aux = 64 if e == 0 else 0
            own = (lane1 < 64) if e == 0 else (lane1 >= 64)
            own_m = low(own.astype(F32))
            first = low((lane1 == aux).astype(F32))
            ka = kp * own_m + bias * first
            va = vp * own_m + first
            qx = qp * own_m + first
            s = dot(qx, ka, NT)
            m = jnp.max(s, axis=1, keepdims=True)
            w = low(jnp.exp(s - m))
            oa = dot(w, va)
            total = oa[:, aux:aux + 1]
            outs.append(oa * (1.0 / total))
            hi, mid, lo = split3(m + jnp.log(total))
            tail = jnp.where(lane_q == aux, 1.0, jnp.where(lane_q == aux + 1, -hi, jnp.where(
                lane_q == aux + 2, -mid, jnp.where(lane_q == aux + 3, -lo, 0.0))))
            qa[2 * p + e] = qp * own_m + low(tail)
        o_ref[p] = jnp.where(lane_q < 64, outs[0], outs[1])
        return 0

    lax.fori_loop(0, pairs, pair_step, 0)

    arrive(g_ref, gm, rg)
    pieces(x_ref, xm, sx, rx, False)
    pieces(g_ref, gm, sg, rg, False)


def attend(x, g, lens, w_qkv, b_qkv, nb, hp, blk_len):
    d = x.shape[-1]
    rows = nb * hp
    pairs = d // 128
    out = [
        jax.ShapeDtypeStruct((nb, hp, d), BF16),
        jax.ShapeDtypeStruct((nb, hp, d), BF16),
        jax.ShapeDtypeStruct((H, rows, 128), BF16),
        jax.ShapeDtypeStruct((pairs, 2, rows, 128), BF16),
        jax.ShapeDtypeStruct((pairs, 2, rows, 128), BF16),
        jax.ShapeDtypeStruct((2 * rows, 128), BF16),
        jax.ShapeDtypeStruct((pairs, rows, 128), F32),
    ]
    dma = pltpu.SemaphoreType.DMA
    return pl.pallas_call(
        functools.partial(attend_kernel, (nb, hp, blk_len, d)),
        name="attend",
        out_shape=out,
        in_specs=[VM, VM, VM, ANY, VM],
        out_specs=[VM] * len(out),
        scratch_shapes=[
            VMEM(w_qkv.shape, BF16),
            VMEM((2, 2, 8, 128), F32),
            VMEM((pairs, rows, 128), BF16),
            dma, dma((4,)), dma((nb,)), dma((4,)), dma((nb,)), dma((2,)), dma((2,)), dma((2,)),
        ],
        compiler_params=pltpu.CompilerParams(collective_id=0, has_side_effects=True, vmem_limit_bytes=60 << 20),
    )(x, g, lens, w_qkv, b_qkv)
def norm(v, gain, shift):
    mean = jnp.mean(v, axis=1, keepdims=True)
    cen = v - mean
    inv = lax.rsqrt(jnp.mean(cen * cen, axis=1, keepdims=True) + EPS)
    n = cen * inv
    return n * gain + shift, n, inv


def norm_back(up, n, inv, gain):
    s = up * gain
    return inv * (s - jnp.mean(s, axis=1, keepdims=True) - n * jnp.mean(s * n, axis=1, keepdims=True))


def total(v):
    return jnp.sum(v, axis=0, keepdims=True)


FC = 512


def rows_kernel(xm, gm, o_ref, vec, bup, wo_hbm, wu_hbm, wd_hbm,
                out_ref, gh_ref, da_ref, gvec, gbup, gwo_ref, gwu_hbm, gwd_hbm,
                wo, wu, wd, ab, act, fac, n1_s, gs2, acc, stage_u, stage_d, sems, osem):
    rows, d = n1_s.shape
    chunks = act.shape[0]
    pairs = d // 128
    cw = pltpu.make_async_copy(wo_hbm, wo, sems.at[0])
    cu = pltpu.make_async_copy(wu_hbm, wu, sems.at[1])
    cd = pltpu.make_async_copy(wd_hbm, wd, sems.at[2])
    cw.start()
    cu.start()
    cd.start()
    bias_out, gain1, shift1, bias_down, gain2, shift2 = (vec[i:i + 1, :] for i in range(6))
    for p in range(pairs):
        ab[:, 128 * p:128 * p + 128] = low(o_ref[p])
    x = xm[...].reshape(rows, d).astype(F32)
    cw.wait()
    hidden = x + dot(ab[...], wo[...]) + bias_out
    normed, n1, inv1 = norm(hidden, gain1, shift1)
    n1_s[...] = n1
    acc[...] = normed + bias_down
    nl = low(normed)
    cu.wait()
    cd.wait()

    def up_step(j, _):
        at = pl.ds(pl.multiple_of(j * FC, FC), FC)
        u = dot(nl, wu[:, at]) + bup[:, at]
        cdf = 0.5 + 0.5 * lax.erf(u * 0.7071067811865476)
        dens = jnp.exp(-0.5 * u * u) * 0.3989422804014327
        a = low(u * cdf)
        act[j] = a
        fac[j] = cdf + u * dens
        acc[...] += dot(a, wd[at, :])
        return 0

    lax.fori_loop(0, chunks, up_step, 0)
    result, n2, inv2 = norm(acc[...], gain2, shift2)
    out_ref[...] = low(result).reshape(out_ref.shape)
    g = gm[...].reshape(rows, d).astype(F32)
    gvec[0:1, :] = total(g * n2)
    gvec[1:2, :] = total(g)
    back2 = norm_back(g, n2, inv2, gain2)
    gs2[...] = back2
    gb = low(back2)
    gvec[2:3, :] = total(gb.astype(F32))
    gbt = gb.T
    nt = nl.T

    acc[...] = back2

    def down_step(j, _):
        at = pl.ds(pl.multiple_of(j * FC, FC), FC)
        ga = dot(gb, wd[at, :], NT)
        gu32 = ga * fac[j]
        gu = low(gu32)
        gbup[:, at] = total(gu.astype(F32))
        acc[...] += dot(gu, wu[:, at], NT)
        stage_d[j] = low(dot(gbt, act[j]))
        stage_u[j] = low(dot(nt, gu))
        pltpu.make_async_copy(stage_d.at[j], gwd_hbm.at[:, at], osem.at[0, j]).start()
        pltpu.make_async_copy(stage_u.at[j], gwu_hbm.at[:, at], osem.at[1, j]).start()
        return 0

    lax.fori_loop(0, chunks, down_step, 0)
    gn = acc[...]
    n1 = n1_s[...]
    gvec[3:4, :] = total(gn * n1)
    gvec[4:5, :] = total(gn)
    gh = norm_back(gn, n1, inv1, gain1)
    gh_ref[...] = gh
    ga = low(gh)
    gvec[5:6, :] = total(ga.astype(F32))
    gvec[6:8, :] = jnp.zeros((2, d), F32)
    at = low(ab[...])
    gwo_ref[...] = low(dot(at.T, ga))
    datt = low(dot(ga, wo[...], NT))
    lane = lane_of((rows, 128))
    for p in range(pairs):
        dp_ = datt[:, 128 * p:128 * p + 128]
        prod = dp_.astype(F32) * o_ref[p]
        for e in range(2):
            aux = 64 if e == 0 else 0
            own = (lane < 64) if e == 0 else (lane >= 64)
            dd = jnp.sum(jnp.where(own, prod, 0.0), axis=1, keepdims=True)
            hi, mid, lo = split3(dd)
            tail = jnp.where(lane == aux, -hi, jnp.where(lane == aux + 1, -mid, jnp.where(lane == aux + 2, -lo, 0.0)))
            da_ref[2 * p + e] = low(jnp.where(own, dp_.astype(F32), tail))
    for j in range(chunks):
        at = pl.ds(j * FC, FC)
        pltpu.make_async_copy(stage_d.at[j], gwd_hbm.at[:, at], osem.at[0, j]).wait()
        pltpu.make_async_copy(stage_u.at[j], gwu_hbm.at[:, at], osem.at[1, j]).wait()


def rows_pass(xm, gm, o, vec, bup, w_out, w_up, w_down):
    nb, hp, d = xm.shape
    rows = nb * hp
    ff = w_up.shape[1]
    chunks = ff // FC
    out = [
        jax.ShapeDtypeStruct((nb, hp, d), BF16),
        jax.ShapeDtypeStruct((rows, d), F32),
        jax.ShapeDtypeStruct((H, rows, 128), BF16),
        jax.ShapeDtypeStruct((8, d), F32),
        jax.ShapeDtypeStruct((1, ff), F32),
        jax.ShapeDtypeStruct((d, d), BF16),
        jax.ShapeDtypeStruct((d, ff), BF16),
        jax.ShapeDtypeStruct((d, ff), BF16),
    ]
    dma = pltpu.SemaphoreType.DMA
    return pl.pallas_call(
        rows_kernel,
        name="rows_pass",
        out_shape=out,
        in_specs=[VM] * 5 + [ANY] * 3,
        out_specs=[VM] * 6 + [ANY] * 2,
        scratch_shapes=[
            VMEM(w_out.shape, BF16), VMEM(w_up.shape, BF16), VMEM(w_down.shape, BF16),
            VMEM((rows, d), BF16), VMEM((chunks, rows, FC), BF16), VMEM((chunks, rows, FC), F32),
            VMEM((rows, d), F32), VMEM((rows, d), F32), VMEM((rows, d), F32),
            VMEM((chunks, d, FC), BF16), VMEM((chunks, d, FC), BF16),
            dma((3,)), dma((2, chunks)),
        ],
        compiler_params=pltpu.CompilerParams(vmem_limit_bytes=60 << 20),
    )(xm, gm, o, vec, bup, w_out, w_up, w_down)
def bit_of(v, k):
    return lax.rem(lax.div(v, 1 << k), 2)


def flip(v, k):
    return v + (1 << k) - (2 << k) * bit_of(v, k)


class Sum:
    def __init__(self, where, order, src, part, own, r0, r1, r2, rx, zs, rz, sems, piece, own_ready=None):
        self.dp, self.z, self.nbits, self.nb = where
        self.order, self.src, self.part = order, src, part
        self.own, self.r0, self.r1, self.r2, self.rx, self.zs, self.rz = own, r0, r1, r2, rx, zs, rz
        self.sems, self.piece = sems, piece
        low_bit = self.nbits - 3
        self.bits = [low_bit + k for k in order]
        self.mine = [bit_of(self.dp, t) for t in self.bits]
        self.extra = list(range(low_bit))

    def remote(self, src, dst, n, to):
        return pltpu.make_async_remote_copy(src_ref=src, dst_ref=dst, send_sem=self.sems.at[0, n],
                                            recv_sem=self.sems.at[1, n], device_id=to, device_id_type=MESH)

    def index(self, first, a, b):
        k0, k1, k2 = self.order
        return (first << k0) + (a << k1) + (b << k2) if not isinstance(first, int) else None

    def part_at(self, m0, a, b):
        k0, k1, k2 = self.order
        return m0 * (1 << k0) + a * (1 << k1) + b * (1 << k2)

    def copies(self, stage):
        to = (flip(self.dp, self.bits[stage]), self.z)
        m = self.mine
        if stage == 0:
            return [self.remote(self.part(self.src, self.part_at(1 - m[0], a, b)), self.r0.at[a, b], 2 * a + b, to)
                    for a in range(2) for b in range(2)]
        if stage == 1:
            return [self.remote(self.r0.at[1 - m[1]], self.r1, 4, to)]
        return [self.remote(self.r0.at[m[1], 1 - m[2]], self.r2, 5, to)]

    def local(self):
        m = self.mine
        return [pltpu.make_async_copy(self.part(self.src, self.part_at(m[0], a, b)), self.own.at[a, b],
                                      self.sems.at[0, 8 + 2 * a + b]) for a in range(2) for b in range(2)]

    def start(self):
        for c in self.copies(0):
            c.start()
        for c in self.local():
            c.start()

    def next1(self):
        for c in self.local():
            c.wait()
        for c in self.copies(0):
            c.wait()
        m1 = self.mine[1]
        self.r0[1 - m1] = self.r0[1 - m1] + self.own[1 - m1]
        for c in self.copies(1):
            c.start()
        self.r0[m1] = self.r0[m1] + self.own[m1]

    def next2(self):
        for c in self.copies(1):
            c.wait()
        m1, m2 = self.mine[1:]
        self.r0[m1, 1 - m2] = self.r0[m1, 1 - m2] + self.r1[1 - m2]
        for c in self.copies(2):
            c.start()
        self.r0[m1, m2] = self.r0[m1, m2] + self.r1[m2]

    def pieces(self):
        out = []
        for dz in range(1, self.nb):
            to = lax.rem(self.z + dz, self.nb)
            out.append(self.remote(self.zs.at[to], self.rz.at[self.z], 12 + dz, (self.dp, to)))
        return out

    def landed(self):
        for dz in range(1, self.nb):
            frm = lax.rem(self.z + self.nb - dz, self.nb)
            self.remote(self.zs.at[frm], self.rz.at[frm], 12 + dz, (self.dp, frm)).wait_recv()

    def next3(self):
        for c in self.copies(2):
            c.wait()
        m1, m2 = self.mine[1:]
        v = self.r0[m1, m2].astype(F32) + self.r2[...].astype(F32)
        for n, t in enumerate(self.extra):
            self.r2[...] = low(v)
            c = self.remote(self.r2, self.rx.at[n], 16 + n, (flip(self.dp, t), self.z))
            c.start()
            c.wait()
            v = v + self.rx[n].astype(F32)
        self.piece(self.zs, low(v))
        for c in self.pieces():
            c.start()

    def finish(self):
        self.landed()
        for c in self.pieces():
            c.wait_send()
        v = self.zs[self.z].astype(F32)
        for dz in range(1, self.nb):
            v = v + self.rz[lax.rem(self.z + dz, self.nb)].astype(F32)
        return v


def grads_kernel(geo, xm, om, qa, kall, vall, kb, da, gh, gvec, gbup, gwo, wq_hbm, gwd_hbm, gwu_hbm,
                 out_z, dx_z, fd, fu, fq, fv,
                 wq, gq, dqkv, kvown, kvsend, kvrecv, dxs,
                 owd, r0d, r1d, r2d, rxd, zsd, rzd,
                 owu, r0u, r1u, r2u, rxu, zsu, rzu,
                 r0a, r1a, r2a, rxa, zsa, rza,
                 r0b, r1b, r2b, rxb, zsb, rzb,
                 rv, wsem, sd, su, sa, sb, so, ro, sx, rx, skv, rkv, sv):
    nb, hp, nbits = geo
    dp, z, c = place()
    base = dp - c
    peer = (base + 1 - c, z)
    rows, d = gh.shape
    pairs = d // 128
    wcopy = pltpu.make_async_copy(wq_hbm, wq, wsem)
    wcopy.start()

    barrier = pltpu.get_barrier_semaphore()
    count = 0
    for dz in range(nb):
        for dc in range(2):
            if dz or dc:
                pl.semaphore_signal(barrier, inc=1, device_id=(base + lax.rem(c + dc, 2), lax.rem(z + dz, nb)),
                                    device_id_type=MESH)
                count += 1
    for t in range(1, nbits):
        pl.semaphore_signal(barrier, inc=1, device_id=(flip(dp, t), z), device_id_type=MESH)
        count += 1
    pl.semaphore_wait(barrier, count)

    def back(src, dst, ss, rs, start):
        for b in range(nb):
            to_c = lax.div(z, 2)
            here = jnp.logical_and(z == b, c == to_c)
            land = dst.at[lax.rem(z, 2), pl.ds(pl.multiple_of(c * hp, 16), hp)]
            n = 2 * lax.rem(z, 2) + c
            remote = pltpu.make_async_remote_copy(src_ref=src.at[b], dst_ref=land, send_sem=ss.at[b],
                                                  recv_sem=rs.at[n], device_id=(base + to_c, jnp.int32(b)),
                                                  device_id_type=MESH)

            @pl.when(jnp.logical_not(here))
            def _():
                remote.start() if start else remote.wait_send()

            if start:
                @pl.when(here)
                def _():
                    pltpu.make_async_copy(src.at[b], land, rs.at[n]).start()

    def arrive(src, dst, rs):
        for n in range(4):
            pltpu.make_async_copy(src.at[0], dst.at[n // 2, pl.ds((n % 2) * hp, hp)], rs.at[n]).wait()

    where = (dp, z, nbits, nb)
    part_r = d // 8
    part_f = gwd_hbm.shape[1] // 8
    row_part = lambda ref, p: ref.at[pl.ds(pl.multiple_of(p * part_r, 16), part_r), :]
    col_part = lambda ref, p: ref.at[:, pl.ds(pl.multiple_of(p * part_f, 128), part_f)]

    def row_pieces(zs, v):
        n = v.shape[0] // nb
        for j in range(nb):
            zs[j] = v[n * j:n * j + n, :]

    def col_pieces(zs, v):
        n = v.shape[1] // nb
        for j in range(nb):
            zs[j] = v[:, n * j:n * j + n]

    def whole(zs, v):
        zs[0] = v

    jd = Sum(where, (0, 1, 2), gwd_hbm, col_part, owd, r0d, r1d, r2d, rxd, zsd, rzd, sd, row_pieces)
    ju = Sum(where, (0, 2, 1), gwu_hbm, row_part, owu, r0u, r1u, r2u, rxu, zsu, rzu, su, col_pieces)
    jd.start()
    ju.start()
    back(om, out_z, so, ro, True)

    gq[:, 3 * d:4 * d] = gwo[...]
    lane1 = lane_of((1, 128))
    lane = lane_of((rows, 128))

    def kvcopy(p):
        return pltpu.make_async_remote_copy(src_ref=kvsend.at[p], dst_ref=kvrecv.at[p], send_sem=skv.at[p],
                                            recv_sem=rkv.at[p], device_id=peer, device_id_type=MESH)

    def pair_step(p, _):
        @pl.when(p == 1)
        def _():
            jd.next1()
            ju.next1()

        @pl.when(p == pairs - 1)
        def _():
            jd.next2()
            ju.next2()

        dq = [None, None]
        for n in range(2):
            h = (1 - c) if n == 0 else c
            kp = kall[p, h]
            vp = vall[p, h]
            bias = kb[pl.ds(pl.multiple_of(h * rows, 16), rows), :]
            kt = kp.T
            dks, dvs = [], []
            for e in range(2):
                aux = 64 if e == 0 else 0
                own = (lane1 < 64) if e == 0 else (lane1 >= 64)
                own_m = low(own.astype(F32))
                first = low((lane1 == aux).astype(F32))
                ones = lambda lo, hi: low(jnp.logical_and(lane1 >= aux + lo, lane1 <= aux + hi).astype(F32))
                kx = kp * own_m + (bias * first + ones(1, 3))
                vx = vp * own_m + ones(0, 2)
                q = qa[2 * p + e]
                do = da[2 * p + e]
                pt = jnp.exp(dot(kx, q, NT))
                ds = low(pt * dot(vx, do, NT))
                dvs.append(dot(low(pt), do))
                dks.append(dot(ds, q))
                t = dot(kt[64 * e:64 * e + 64, :], ds)
                dq[e] = t if dq[e] is None else dq[e] + t
            dk = jnp.where(lane < 64, dks[0], dks[1])
            dv = jnp.where(lane < 64, dvs[0], dvs[1])
            if n == 0:
                kvsend[p, 0] = low(dk)
                kvsend[p, 1] = low(dv)
                kvcopy(p).start()
            else:
                kvown[p, 0] = dk
                kvown[p, 1] = dv
        dqp = jnp.concatenate(dq, axis=0).T * 0.125
        dqkv[:, pl.ds(pl.multiple_of(p * 128, 128), 128)] = low(dqp)
        return 0

    lax.fori_loop(0, pairs, pair_step, 0)
    for p in range(pairs):
        kvcopy(p).wait()
        for n in range(2):
            at = (n + 1) * d + 128 * p
            dqkv[:, at:at + 128] = low(kvown[p, n] + kvrecv[p, n].astype(F32))

    xt = xm[...].reshape(rows, d).T
    for j in range(3 * d // 256):
        gq[:, 256 * j:256 * j + 256] = low(dot(xt, dqkv[:, 256 * j:256 * j + 256]))
    half = gq.shape[1] // 2
    row_part_a = lambda ref, p: ref.at[pl.ds(pl.multiple_of(p * part_r, 16), part_r), pl.ds(0, half)]
    row_part_b = lambda ref, p: ref.at[pl.ds(pl.multiple_of(p * part_r, 16), part_r), pl.ds(half, half)]

    class Held(Sum):
        def local(self):
            return []

        def add(self, at):
            self.r0[at] = self.r0[at]

        def next1(self):
            for cc in self.copies(0):
                cc.wait()
            m = self.mine

            def grow(a):
                for b in range(2):
                    own = self.part(self.src, self.part_at(m[0], a, b))
                    self.r0[a, b] = self.r0[a, b] + own[...]
            grow(1 - m[1])
            for cc in self.copies(1):
                cc.start()
            grow(m[1])

    ja = Held(where, (0, 1, 2), gq, row_part_a, None, r0a, r1a, r2a, rxa, None, None, sa, None)
    jb = Held(where, (0, 2, 1), gq, row_part_b, None, r0b, r1b, r2b, rxb, None, None, sb, None)
    ja.start()
    jb.start()

    vec = fv
    vec[0:8, :] = gvec[...]
    for i in range(gbup.shape[1] // d):
        vec[8 + i:9 + i, :] = gbup[:, d * i:d * i + d]
    vec[12:13, :] = total(dqkv[:, 0:d].astype(F32))
    vec[13:14, :] = total(dqkv[:, 2 * d:3 * d].astype(F32))
    vec[14:16, :] = jnp.zeros((2, d), F32)

    wcopy.wait()
    dx = low(gh[...] + dot(dqkv[...], wq[...], NT))
    dxs[...] = dx.reshape(dxs.shape)
    back(dxs, dx_z, sx, rx, True)

    jd.next3()
    ju.next3()
    ja.next1()
    jb.next1()

    steps = [((flip(dp, t), z), t) for t in range(nbits)] + [((dp, flip(z, t)), nbits + t) for t in range(2)]
    for to, n in steps:
        cp = pltpu.make_async_remote_copy(src_ref=vec, dst_ref=rv.at[n], send_sem=sv.at[0, n], recv_sem=sv.at[1, n],
                                          device_id=to, device_id_type=MESH)
        cp.start()
        cp.wait()
        vec[...] += rv[n]

    ja.next2()
    jb.next2()
    fd[...] = jd.finish()
    fu[...] = ju.finish()

    def last(job):
        for cc in job.copies(2):
            cc.wait()
        m1, m2 = job.mine[1:]
        v = job.r0[m1, m2].astype(F32) + job.r2[...].astype(F32)
        for n, t in enumerate(job.extra):
            job.r2[...] = low(v)
            cp = job.remote(job.r2, job.rx.at[n], 16 + n, (flip(dp, t), z))
            cp.start()
            cp.wait()
            v = v + job.rx[n].astype(F32)
        return v

    va, vb = last(ja), last(jb)
    v = jnp.concatenate([va, vb], axis=1)

    def cut(zs, v):
        wq_, wo_ = 3 * d // nb, d // nb
        rolled = pltpu.roll(v, v.shape[1] - 64, 1)
        for j in range(nb):
            at = 0
            for first, w in ((0, wq_), (3 * d, wo_)):
                s0 = first + w * j
                r = s0 % 128
                wide = -(-w // 128) * 128
                zs[j, :, at:at + wide] = low((rolled if r else v)[:, s0 - r:s0 - r + wide])
                at += wide
    jz = Sum(where, (0, 1, 2), None, None, None, None, None, None, None, zsa, rza, sa, None)
    cut(zsa, v)
    for cc in jz.pieces():
        cc.start()
    fq[...] = jz.finish()

    back(om, out_z, so, ro, False)
    arrive(om, out_z, ro)
    back(dxs, dx_z, sx, rx, False)
    arrive(dxs, dx_z, rx)


def grads(nbits, xm, om, qa, kall, vall, kb, da, gh, gvec, gbup, gwo, w_qkv, gwd, gwu):
    nb, hp, d = xm.shape
    rows = nb * hp
    pairs = d // 128
    ff = gwd.shape[1]
    pr, pf = d // 8, ff // 8
    wide = -(-(3 * d // nb) // 128) * 128 + -(-(d // nb) // 128) * 128
    extra = max(nbits - 3, 1)
    out = [
        jax.ShapeDtypeStruct((2, 2 * hp, d), BF16),
        jax.ShapeDtypeStruct((2, 2 * hp, d), BF16),
        jax.ShapeDtypeStruct((d // nb, pf), F32),
        jax.ShapeDtypeStruct((pr, ff // nb), F32),
        jax.ShapeDtypeStruct((pr, wide), F32),
        jax.ShapeDtypeStruct((16, d), F32),
    ]
    dma = pltpu.SemaphoreType.DMA

    def job(r, c, own, pieces):
        got = [VMEM((2, 2, r, c), BF16)] if own else []
        got += [VMEM((2, 2, r, c), BF16), VMEM((2, r, c), BF16), VMEM((r, c), BF16), VMEM((extra, r, c), BF16)]
        return got + [VMEM((nb,) + pieces, BF16)] * 2
    scratch = [
        VMEM(w_qkv.shape, BF16), VMEM((d, 4 * d), BF16), VMEM((rows, 3 * d), BF16),
        VMEM((pairs, 2, rows, 128), F32), VMEM((pairs, 2, rows, 128), BF16), VMEM((pairs, 2, rows, 128), BF16),
        VMEM((nb, hp, d), BF16),
    ]
    scratch += job(d, pf, True, (d // nb, pf)) + job(pr, ff, True, (pr, ff // nb))
    scratch += job(pr, 2 * d, False, (pr, wide)) + job(pr, 2 * d, False, (8, 128))
    scratch += [VMEM((nbits + 2, 16, d), F32), dma] + [dma((2, 16 + extra))] * 4
    scratch += [dma((nb,)), dma((4,)), dma((nb,)), dma((4,)), dma((pairs,)), dma((pairs,)), dma((2, nbits + 2))]
    return pl.pallas_call(
        functools.partial(grads_kernel, (nb, hp, nbits)),
        name="grads",
        out_shape=out,
        in_specs=[VM] * 11 + [ANY] * 3,
        out_specs=[VM] * len(out),
        scratch_shapes=scratch,
        compiler_params=pltpu.CompilerParams(collective_id=1, has_side_effects=True, vmem_limit_bytes=60 << 20),
    )(xm, om, qa, kall, vall, kb, da, gh, gvec, gbup, gwo, w_qkv, gwd, gwu)
def shards(speech, lengths, grad_output, w_qkv, bias_query, bias_value, w_out, bias_out, gain_first, shift_first,
           w_up, bias_up, w_down, bias_down, gain_second, shift_second):
    utts, blk_len, d = speech.shape
    nb = lax.axis_size("blk")
    ndp = lax.axis_size("dp")
    nbits = ndp.bit_length() - 1
    hp = -(-blk_len // 32) * 16
    fill = ((0, 0), (0, 2 * hp - blk_len), (0, 0))
    lens = jnp.broadcast_to(lengths.astype(F32)[:, None, None], (utts, 8, 128))
    b_qkv = jnp.concatenate([bias_query, jnp.zeros_like(bias_query), bias_value])[None]
    vec = jnp.stack([bias_out, gain_first, shift_first, bias_down, gain_second, shift_second])
    xm, gm, qa, kall, vall, kb, o = attend(jnp.pad(speech, fill), jnp.pad(grad_output, fill), lens, w_qkv, b_qkv,
                                           nb, hp, blk_len)
    om, gh, da, gvec, gbup, gwo, gwu, gwd = rows_pass(xm, gm, o, vec, bias_up[None], w_out, w_up, w_down)
    out_z, dx_z, fd, fu, fq, fv = grads(nbits, xm, om, qa, kall, vall, kb, da, gh, gvec, gbup, gwo, w_qkv, gwd, gwu)
    dp = lax.axis_index("dp")
    parts = ndp // 8
    sub = lax.rem(dp, parts)

    def mine(v, axis):
        if parts == 1:
            return v
        n = v.shape[axis] // parts
        return lax.dynamic_slice_in_dim(v, sub * n, n, axis)

    wq, wo = 3 * d // nb, d // nb
    at = -(-wq // 128) * 128
    ff = bias_up.shape[0]
    return (
        out_z[:, :blk_len],
        dx_z[:, :blk_len].astype(F32),
        mine(fq[:, :wq], 0),
        fv[12],
        fv[13],
        mine(fq[:, at:at + wo], 0),
        fv[5],
        fv[3],
        fv[4],
        mine(fu, 0),
        fv[8:8 + ff // d].reshape(ff),
        mine(fd.T, 0),
        fv[2],
        fv[0],
        fv[1],
    )


def solution(mesh):
    rows = P("dp", "blk", None)
    cut = P("dp", "blk")
    return jax.shard_map(
        shards,
        mesh=mesh,
        in_specs=(rows, P("dp"), rows) + (P(),) * 13,
        out_specs=(rows, rows, cut, P(), P(), cut, P(), P(), P(), cut, P(), cut, P(), P(), P()),
        check_vma=False,
    )
```

time: 582 us -> 211 us (0.36); the launches traced: 571 us -> 210 us
  Pallas kernels: 0 us -> 191 us
  waiting for transfers between devices: 176 us -> 0 us
  matrix products: 150 us -> 0 us
  local copies, waits for them, and re-layouts: 132 us -> 15.8 us
  other arithmetic: 53.1 us -> 2.58 us
  blocking collectives: 40.3 us -> 0 us
  between operations: 15.5 us -> 0.72 us
    pallas_call x0 -> x3, Pallas kernels: none -> 191 us  [the longest x1 123 us: grads(): pl.pallas_call(functools.partial(grads_kernel, (nb, hp, nbits)), name='gr...]
    dot_general x36 -> x0, matrix products: 150 us -> none  [the longest x4 20.8 us: shards(): jnp.einsum('uhqk,uqhd->ukhd', probabilities.astype(jnp.bfloat16), grad_he...]
    ppermute x7 -> x0, waiting for transfers between devices: 85.1 us -> none  [shifted(): return lax.ppermute(block, axis, route)]
    unnamed x11 -> x0, waiting for transfers between devices: 77.6 us -> none
    psum x1 -> x0, blocking collectives: 40.3 us -> none  [shards(): lax.psum((grad_bias_query, grad_bias_value, grad_bias_out, grad_gain_firs...]
    slice x14 -> x5, local copies, waits for them, and re-layouts: 41.3 us -> 4.82 us  [the longest x1 2.06 us: shards(): out_z[:, :blk_len]]
    unnamed x167 -> x14, local copies, waits for them, and re-layouts: 30 us -> 1.45 us
    convert_element_type x6 -> x0, local copies, waits for them, and re-layouts: 23.2 us -> none  [the longest x2 13.4 us: shards(): attended_low = attended_low.astype(jnp.bfloat16)]
  transfers between devices with their start and end apart: 15 -> 0, of which waited for: 10 -> 0; matrix products, arithmetic and copies ran while one was open for 41% -> 0% of each run, Pallas kernels for 0% -> 0%
where the time goes in v1:
time: 211 us; the launch traced here: 210 us
  Pallas kernels  191 us (91%)
  local copies, waits for them, and re-layouts  15.8 us (7%)
  other arithmetic  2.58 us (1%)
    pallas_call x1, Pallas kernels, grads(): pl.pallas_call(functools.partial(grads_kernel, (nb, hp, nbits)), name='gr...  123 us
    pallas_call x1, Pallas kernels, attend(): pl.pallas_call(functools.partial(attend_kernel, (nb, hp, blk_len, d)), na...  37.3 us
    pallas_call x1, Pallas kernels, rows_pass(): pl.pallas_call(rows_kernel, name='rows_pass', out_shape=out, in_specs=[VM...  30.7 us
    another operation x7, local copies, waits for them, and re-layouts, shards(): jnp.stack([bias_out, gain_first, shift_first, bias_down, gain_second, shi...  4.77 us

profile of v1, /device:TPU:0, one launch (start us, length us, event | category | flops | bytes accessed | tf_op | source)
XLA Modules:
  0.0 209.8 jit_solution(10531869013194114005)
XLA Ops:
  0.6 0.0 copy-start
  0.7 0.7 convert_element_type.9
  1.4 0.7 stack.21
  2.1 0.7 stack.22
  2.8 0.7 stack.23
  3.4 0.7 stack.24
  4.1 0.7 stack.25
  4.8 0.7 stack.26
  5.5 0.6 stack.27.vec
  6.2 0.7 broadcast_in_dim.15.lens_ref
  6.8 0.7 pad_maximum_fusion
  7.5 0.6 broadcast_in_dim.17.b_ref
  8.1 2.0 pad.7.x_ref
  10.1 0.0 copy-done
  10.1 0.9 pad.8.g_ref
  11.0 37.3 %attend.1 = (bf16[4,112,768]{2,1,0:T(8,128)(2,1)}, bf16[4,112,768]{2,1,0:T(8,128)(2,1)}, bf16[12,448,128]{2,1,0:T(8,128)(2,1)}, bf16[6,2,448,128]{3,2,1,0:T(8,12...) custom-call(bf16[2,224,768]{2,1,0:T(8,128)(2,1)} %pad.7.x_ref, ...), custom_call_target="tpu_custom_call" | custom-call | tf_op jit(solution)/shard_map/attend/pallas_call | solution.py:180
  48.3 30.7 %rows_pass.1 = (bf16[4,112,768]{2,1,0:T(8,128)(2,1)}, f32[448,768]{1,0:T(8,128)}, bf16[12,448,128]{2,1,0:T(8,128)(2,1)}, f32[8,768]{1,0:T(8,128)}, f32[1,3072]{1...) custom-call(bf16[4,112,768]{2,1,0:T(8,128)(2,1)} %get-tuple-element.36.xm, ...), custom_call_target="tpu_custom_call" | custom-call | tf_op jit(solution)/shard_map/rows_pass/pallas_call | solution.py:324
  79.0 122.8 %grads.1 = (bf16[2,224,768]{2,1,0:T(8,128)(2,1)}, bf16[2,224,768]{2,1,0:T(8,128)(2,1)}, f32[192,384]{1,0:T(8,128)}, f32[96,768]{1,0:T(8,128)}, f32[96,896]{1,0:T(8,128)}, /*index=5*/f32[16,768]{1,0:T(8,128)}) custom-call(bf16[4,112,768]{2,1,0:T(8,128)(2,1)} %get-tuple-element.36.xm, bf16[4,112,768]{2,1,0:T(8,128)(2,1)} %get-tuple-element.39.om, ...), custom_call_target="tpu_custom_call" | custom-call | tf_op jit(solution)/shard_map/grads/pallas_call | solution.py:723
  201.8 0.0 copy-start.5
  201.8 0.0 copy-start.2
  201.8 0.0 copy-start.1
  201.8 2.1 slice.39
  203.9 0.7 slice.48
  204.6 0.0 copy-done.5
  204.6 0.0 copy-start.4
  204.6 0.7 slice_reduce_fusion
  205.3 0.6 reshape.34
  205.9 0.0 copy-done.2
  205.9 0.6 slice.44
  206.5 0.7 slice.41
  207.3 0.0 copy-done.1
  207.3 0.0 copy-start.3
  207.3 1.1 slice_convert_fusion
  208.4 0.0 copy-done.4
  208.4 0.7 copy.33
  209.1 0.0 copy-done.3
  209.1 0.7 copy.34
  (1 shorter events, 0.0 us)
Async XLA Ops:
  0.6 9.5 %copy-start = (bf16[2,216,768]{2,1,0:T(8,128)(2,1)S(1)}, bf16[2,216,768]{2,1,0:T(8,128)(2,1)}, u32[]{:S(2)}) copy-start(bf16[2,216,768]{2,1,0:T(8,128)(2,1)} %param.18) | copy-start | bytes 1990660
  201.8 2.8 %copy-start.5 = (f32[16,768]{1,0:T(8,128)S(1)}, f32[16,768]{1,0:T(8,128)}, u32[]{:S(2)}) copy-start(f32[16,768]{1,0:T(8,128)} %get-tuple-element.54) | copy-start | bytes 147460
  201.8 4.1 %copy-start.2 = (f32[96,896]{1,0:T(8,128)S(1)}, f32[96,896]{1,0:T(8,128)}, u32[]{:S(2)}) copy-start(f32[96,896]{1,0:T(8,128)} %get-tuple-element.53) | copy-start | bytes 1032196
  201.8 5.4 %copy-start.1 = (bf16[2,224,768]{2,1,0:T(8,128)(2,1)S(1)}, bf16[2,224,768]{2,1,0:T(8,128)(2,1)}, u32[]{:S(2)}) copy-start(bf16[2,224,768]{2,1,0:T(8,128)(2,1)} %get-tuple-element.52) | copy-start | bytes 2064388
  204.6 3.8 %copy-start.4 = (f32[96,768]{1,0:T(8,128)S(1)}, f32[96,768]{1,0:T(8,128)}, u32[]{:S(2)}) copy-start(f32[96,768]{1,0:T(8,128)} %get-tuple-element.89) | copy-start | bytes 884740
  207.3 1.9 copy-start.3

commit v2 on v0

v2 whole, which is shorter than its diff:
```python
import functools

import jax
import jax.numpy as jnp
from jax import lax
from jax.experimental import pallas as pl
from jax.experimental.pallas import tpu as pltpu
from jax.sharding import PartitionSpec as P

MESH = pl.DeviceIdType.MESH
VMEM = pltpu.VMEM
F32, BF16 = jnp.float32, jnp.bfloat16
EPS = 1e-05
MASKED = -1000000000.0
FC = 512
NN = (((1,), (0,)), ((), ()))
NT = (((1,), (1,)), ((), ()))
ANY = pl.BlockSpec(memory_space=pl.ANY)
VM = pl.BlockSpec(memory_space=pltpu.VMEM)


def dot(a, b, dims=NN):
    return lax.dot_general(a, b, dims, preferred_element_type=F32)


def low(v):
    return v.astype(BF16)


def total(v):
    return jnp.sum(v, axis=0, keepdims=True)


def split3(v):
    hi = low(v)
    rest = v - hi.astype(F32)
    mid = low(rest)
    return hi.astype(F32), mid.astype(F32), rest - mid.astype(F32)


def lane_of(shape):
    return lax.broadcasted_iota(jnp.int32, shape, len(shape) - 1)


def bit_of(v, k):
    return lax.rem(lax.div(v, 1 << k), 2)


def flip(v, k):
    return v + (1 << k) - (2 << k) * bit_of(v, k)


def norm(v, gain, shift):
    mean = jnp.mean(v, axis=1, keepdims=True)
    cen = v - mean
    inv = lax.rsqrt(jnp.mean(cen * cen, axis=1, keepdims=True) + EPS)
    n = cen * inv
    return n * gain + shift, n, inv


def norm_back(up, n, inv, gain):
    s = up * gain
    return inv * (s - jnp.mean(s, axis=1, keepdims=True) - n * jnp.mean(s * n, axis=1, keepdims=True))


def link(src, dst, sems, n, to):
    return pltpu.make_async_remote_copy(src_ref=src, dst_ref=dst, send_sem=sems.at[0, n], recv_sem=sems.at[1, n],
                                        device_id=to, device_id_type=MESH)


class Halving:
    def __init__(self, dp, z, nbits, order, part, r0, r1, r2, sems):
        self.dp, self.z, self.order, self.part = dp, z, order, part
        self.r0, self.r1, self.r2, self.sems = r0, r1, r2, sems
        self.bits = [nbits - 3 + k for k in order]
        self.mine = [bit_of(dp, t) for t in self.bits]

    def at(self, m, a, b):
        k0, k1, k2 = self.order
        return self.part(m * (1 << k0) + a * (1 << k1) + b * (1 << k2))

    def copies(self, stage):
        to = (flip(self.dp, self.bits[stage]), self.z)
        m = self.mine
        if stage == 0:
            return [link(self.at(1 - m[0], a, b), self.r0.at[a, b], self.sems, 2 * a + b, to)
                    for a in range(2) for b in range(2)]
        if stage == 1:
            return [link(self.r0.at[1 - m[1]], self.r1, self.sems, 4, to)]
        return [link(self.r0.at[m[1], 1 - m[2]], self.r2, self.sems, 5, to)]

    def start(self):
        for c in self.copies(0):
            c.start()

    def next1(self):
        for c in self.copies(0):
            c.wait()
        m = self.mine
        for a in (1 - m[1], m[1]):
            for b in range(2):
                self.r0[a, b] = self.r0[a, b] + self.at(m[0], a, b)[...]
            if a is not m[1]:
                for c in self.copies(1):
                    c.start()

    def next2(self):
        for c in self.copies(1):
            c.wait()
        m1, m2 = self.mine[1:]
        self.r0[m1, 1 - m2] = self.r0[m1, 1 - m2] + self.r1[1 - m2]
        for c in self.copies(2):
            c.start()
        self.r0[m1, m2] = self.r0[m1, m2] + self.r1[m2]

    def result(self):
        for c in self.copies(2):
            c.wait()
        return self.r0[self.mine[1], self.mine[2]].astype(F32) + self.r2[...].astype(F32)


class Pieces:
    def __init__(self, dp, z, nbits, zs, r1, r2, rx, sems):
        self.zs, self.r1, self.r2, self.rx, self.sems = zs, r1, r2, rx, sems
        self.more = [(flip(dp, t), z) for t in range(nbits - 3)]
        self.b = [bit_of(z, 0), bit_of(z, 1)]
        self.to = [(dp, flip(z, 0)), (dp, flip(z, 1))]

    def first(self):
        return link(self.zs.at[1 - self.b[0]], self.r1, self.sems, 0, self.to[0])

    def second(self):
        return link(self.zs.at[self.b[0], 1 - self.b[1]], self.r2, self.sems, 1, self.to[1])

    def start(self):
        self.first().start()

    def next1(self):
        self.first().wait()
        b0, b1 = self.b
        self.zs[b0, 1 - b1] = self.zs[b0, 1 - b1] + self.r1[1 - b1]
        self.second().start()

    def result(self):
        self.second().wait()
        b0, b1 = self.b
        v = self.zs[b0, b1].astype(F32) + self.r1[b1].astype(F32) + self.r2[...].astype(F32)
        for n, to in enumerate(self.more):
            self.zs[b0, b1] = low(v)
            c = link(self.zs.at[b0, b1], self.rx.at[n], self.sems, 2 + n, to)
            c.start()
            c.wait()
            v = v + self.rx[n].astype(F32)
        return v


def layer_kernel(geo, len_ref, x_ref, g_ref, bq, bv, bo, g1, s1, bu, bd, g2, s2, wq_hbm, wo_hbm, wu_hbm, wd_hbm,
                 out_z, dx_z, fd, fu, fq, fv, *scratch):
    nb, hp, nbits, heads = geo
    (wq, wo, wu, wd, xm, gm, om, qa, kall, vall, kb, o_s, ab, nl, inv1, act, fac, n1_s, acc, gwd, gwu, kvrecv, lens, rv, vhalf, rv2, vec2,
     *rest) = scratch
    jobs, rest = rest[:24], rest[24:]
    zbufs, (wsem, lsem, kvsem, kvs2, vsem, vsem2, sx, rx, sg, rg, so, ro, sd, rd, *jsem) = rest[:12], rest[12:]
    blk_len, d = x_ref.shape[1:]
    dp, z = lax.axis_index("dp"), lax.axis_index("blk")
    c = lax.rem(dp, 2)
    base = dp - c
    peer = (base + 1 - c, z)
    rows, ff = act.shape
    nq = (1 << nbits) // 2
    pairs = d // 128
    chunks = ff // FC
    gq = wu
    da = fac
    dqkv = act
    dxs = gm

    weights = [pltpu.make_async_copy(a, b, wsem.at[n])
               for n, (a, b) in enumerate(((wq_hbm, wq), (wo_hbm, wo), (wu_hbm, wu), (wd_hbm, wd)))]
    weights[0].start()

    barrier = pltpu.get_barrier_semaphore()
    greet = [(base + lax.rem(c + dc, 2), lax.rem(z + dz, nb)) for dz in range(nb) for dc in range(2) if dz or dc]
    greet += [(lax.rem(lax.div(dp, 2) + n, nq) * 2 + c, z) for n in range(1, nq)]
    for to in greet:
        pl.semaphore_signal(barrier, inc=1, device_id=to, device_id_type=MESH)

    for src, dst in ((x_ref, out_z), (g_ref, dx_z)):
        for s in range(2):
            dst[s, 2 * hp - 16:, :] = jnp.zeros((16, d), BF16)
            dst[s, 0:blk_len, :] = src[s]
    for s in range(2):
        lens[c, s] = jnp.full((8, 128), len_ref[s], jnp.int32).astype(F32)
    pl.semaphore_wait(barrier, len(greet))

    lcopy = pltpu.make_async_remote_copy(src_ref=lens.at[c], dst_ref=lens.at[c], send_sem=lsem.at[0],
                                         recv_sem=lsem.at[1], device_id=peer, device_id_type=MESH)

    def spread(src, dst, ss, rs, start):
        for s in range(2):
            for h in range(2):
                to = 2 * c + s
                here = jnp.logical_and(to == z, c == h)
                part = src.at[s, pl.ds(h * hp, hp)]
                remote = pltpu.make_async_remote_copy(
                    src_ref=part, dst_ref=dst.at[z], send_sem=ss.at[2 * s + h], recv_sem=rs.at[z],
                    device_id=(base + h, to), device_id_type=MESH)

                @pl.when(jnp.logical_not(here))
                def _():
                    remote.start() if start else remote.wait_send()

                if start:
                    @pl.when(here)
                    def _():
                        pltpu.make_async_copy(part, dst.at[z], rs.at[z]).start()

    def spread_in(src, dst, rs):
        for i in range(nb):
            pltpu.make_async_copy(src.at[0, pl.ds(0, hp)], dst.at[i], rs.at[i]).wait()

    def back(src, dst, ss, rs, start):
        for b in range(nb):
            to_c = lax.div(z, 2)
            here = jnp.logical_and(z == b, c == to_c)
            land = dst.at[lax.rem(z, 2), pl.ds(pl.multiple_of(c * hp, 16), hp)]
            n = 2 * lax.rem(z, 2) + c
            remote = pltpu.make_async_remote_copy(src_ref=src.at[b], dst_ref=land, send_sem=ss.at[b],
                                                  recv_sem=rs.at[n], device_id=(base + to_c, jnp.int32(b)),
                                                  device_id_type=MESH)

            @pl.when(jnp.logical_not(here))
            def _():
                remote.start() if start else remote.wait_send()

            if start:
                @pl.when(here)
                def _():
                    pltpu.make_async_copy(src.at[b], land, rs.at[n]).start()

    def back_in(src, dst, rs):
        for n in range(4):
            pltpu.make_async_copy(src.at[0], dst.at[n // 2, pl.ds((n % 2) * hp, hp)], rs.at[n]).wait()

    lane1 = lane_of((1, 128))
    lane = lane_of((rows, 128))
    own = [lane1 < 64, lane1 >= 64]
    own_m = [low(o.astype(F32)) for o in own]
    auxes = (64, 0)

    def at_aux(e, lo, hi):
        return low(jnp.logical_and(lane1 >= auxes[e] + lo, lane1 <= auxes[e] + hi).astype(F32))

    row = lambda ref: ref[...].reshape(1, ref.shape[0])

    spread(out_z, xm, sx, rx, True)
    lcopy.start()
    weights[0].wait()
    for w in weights[1:]:
        w.start()
    spread_in(out_z, xm, rx)
    spread(out_z, xm, sx, rx, False)
    spread(dx_z, gm, sg, rg, True)
    x = xm[...].reshape(rows, d)
    kvs = []
    for part, scr in ((1, kall), (2, vall)):
        for p in range(pairs // 2):
            at = part * d + 256 * p
            t = dot(x, wq[:, at:at + 256])
            if part == 2:
                t = t + row(bv)[:, 256 * p:256 * p + 256]
            t = low(t)
            for e in range(2):
                scr[2 * p + e, c] = t[:, 128 * e:128 * e + 128]
        kv = pltpu.make_async_remote_copy(src_ref=scr.at[:, c], dst_ref=scr.at[:, c], send_sem=kvs2.at[0, part - 1],
                                          recv_sem=kvs2.at[1, part - 1], device_id=peer, device_id_type=MESH)
        kv.start()
        kvs.append(kv)
    for p in range(pairs // 2):
        at = 256 * p
        t = low(dot(x, wq[:, at:at + 256]) + row(bq)[:, at:at + 256])
        t = low(t.astype(F32) * 0.125)
        for q in range(2):
            for e in range(2):
                qa[2 * (2 * p + q) + e] = t[:, 128 * q:128 * q + 128] * own_m[e] + at_aux(e, 0, 0)
    lcopy.wait()
    usable_len = lens[lax.div(z, 2), lax.rem(z, 2)][0:1]
    for h in range(2):
        for b in range(nb):
            t = lax.broadcasted_iota(jnp.int32, (hp, 128), 0) + h * hp
            frame = (t + blk_len * b).astype(F32)
            ok = jnp.logical_and(t < blk_len, frame < usable_len)
            kb[pl.ds((h * nb + b) * hp, hp), :] = low(jnp.where(ok, 0.0, MASKED))
    for kv in kvs:
        kv.wait()

    def attend_step(p, _):
        kp = kall[p].reshape(2 * rows, 128)
        vp = vall[p].reshape(2 * rows, 128)
        bias = kb[...]
        outs = []
        for e in range(2):
            aux = auxes[e]
            first = at_aux(e, 0, 0)
            ka = kp * own_m[e] + bias * first
            va = vp * own_m[e] + first
            qx = qa[2 * p + e]
            s = dot(qx, ka, NT)
            m = jnp.max(s, axis=1, keepdims=True)
            oa = dot(low(jnp.exp(s - m)), va)
            tot = oa[:, aux:aux + 1]
            outs.append(oa * (1.0 / tot))
            hi, mid, lo = split3(m + jnp.log(tot))
            tail = jnp.where(lane == aux + 1, -hi, jnp.where(lane == aux + 2, -mid, jnp.where(lane == aux + 3, -lo, 0.0)))
            qa[2 * p + e] = qx + low(tail)
        o_s[p] = jnp.where(lane < 64, outs[0], outs[1])
        return 0

    lax.fori_loop(0, pairs, attend_step, 0)

    for p in range(pairs):
        ab[:, 128 * p:128 * p + 128] = low(o_s[p])
    weights[1].wait()
    acc[...] = dot(ab[...], wo[...])

    def norm1(i, _):
        at = pl.ds(pl.multiple_of(i * hp, 16), hp)
        normed, n, inv = norm(xm[i].astype(F32) + acc[at] + row(bo), row(g1), row(s1))
        n1_s[at] = n
        inv1[at] = jnp.broadcast_to(inv, (hp, 128))
        acc[at] = normed + row(bd)
        nl[at] = low(normed)
        return 0

    lax.fori_loop(0, nb, norm1, 0)
    weights[2].wait()
    weights[3].wait()

    for j in range(chunks):
        at = slice(j * FC, j * FC + FC)
        u = dot(nl[...], wu[:, at]) + row(bu)[:, at]
        cdf = 0.5 + 0.5 * lax.erf(u * 0.7071067811865476)
        dens = jnp.exp(-0.5 * u * u) * 0.3989422804014327
        a = low(u * cdf)
        act[:, at] = a
        fac[:, at] = low(cdf + u * dens)
        acc[...] += dot(a, wd[at, :])
    spread_in(dx_z, gm, rg)
    spread(dx_z, gm, sg, rg, False)
    fv[...] = jnp.zeros(fv.shape, F32)

    def norm2(i, _):
        at = pl.ds(pl.multiple_of(i * hp, 16), hp)
        result, n2, inv2 = norm(acc[at], row(g2), row(s2))
        om[i] = low(result)
        g = gm[i].astype(F32)
        fv[0:1, :] += total(g * n2)
        fv[1:2, :] += total(g)
        back2 = norm_back(g, n2, inv2, row(g2))
        acc[at] = back2
        gb = low(back2)
        fv[2:3, :] += total(gb.astype(F32))
        gm[i] = gb
        return 0

    lax.fori_loop(0, nb, norm2, 0)
    back(om, out_z, so, ro, True)
    gb = gm[...].reshape(rows, d)
    gbt = gb.T

    def make(n, order, part):
        return Halving(dp, z, nbits, order, part, *jobs[3 * n:3 * n + 3], jsem[n])

    pr, pf = d // 8, ff // 8
    hd, hf = d // 2, ff // 2
    rows_of = lambda ref, p, at, n: ref.at[pl.ds(pl.multiple_of(p * pr, 16), pr), pl.ds(at, n)]
    def down_part(i, p):
        if i == 0:
            return gwd.at[:, pl.ds(pl.multiple_of(p * pf, 128), pf)]
        across = wq.shape[1] // pf
        return wq.at[pl.ds(pl.multiple_of(lax.div(p, across) * hd, 16), hd),
                     pl.ds(pl.multiple_of(lax.rem(p, across) * pf, 128), pf)]

    jd = [make(i, ((0, 1, 2), (0, 2, 1))[i], functools.partial(down_part, i)) for i in range(2)]
    ju = [make(2 + i, ((0, 1, 2), (0, 2, 1))[i], functools.partial(
        lambda i, p: rows_of(gwu, p, i * hf, hf), i)) for i in range(2)]
    for i in range(2):
        for p in range(0, 8, 2):
            t = low(dot(gbt[i * hd:i * hd + hd, :], act[:, p * pf:p * pf + 2 * pf]))
            down_part(i, p)[...] = t[:, :pf]
            down_part(i, p + 1)[...] = t[:, pf:]
        jd[i].start()

    nt = nl[...].T
    for j in range(chunks):
        at = slice(j * FC, j * FC + FC)
        gu = low(dot(gb, wd[at, :], NT) * fac[:, at].astype(F32))
        bup = total(gu.astype(F32))
        for i in range(FC // 128):
            k = j * FC + 128 * i
            fv[8 + k // d:9 + k // d, k % d:k % d + 128] = bup[:, 128 * i:128 * i + 128]
        acc[...] += dot(gu, wu[:, at], NT)
        gwu[:, at] = low(dot(nt, gu))
        if j == 1:
            jd[0].next1()
        if j == 2:
            jd[1].next1()
            ju[0].start()
    ju[1].start()

    def norm1_back(i, _):
        at = pl.ds(pl.multiple_of(i * hp, 16), hp)
        gn = acc[at]
        n1 = n1_s[at]
        fv[3:4, :] += total(gn * n1)
        fv[4:5, :] += total(gn)
        gh = norm_back(gn, n1, inv1[at, 0:1], row(g1))
        n1_s[at] = gh
        ga = low(gh)
        fv[5:6, :] += total(ga.astype(F32))
        nl[at] = ga
        return 0

    lax.fori_loop(0, nb, norm1_back, 0)
    ga = nl[...]
    datt = low(dot(ga, wo[...], NT))
    for p in range(pairs):
        dop = datt[:, 128 * p:128 * p + 128]
        prod = dop.astype(F32) * o_s[p]
        for e in range(2):
            aux = auxes[e]
            hi, mid, lo = split3(jnp.sum(jnp.where(own[e], prod, 0.0), axis=1, keepdims=True))
            tail = jnp.where(lane == aux, -hi, jnp.where(lane == aux + 1, -mid, jnp.where(lane == aux + 2, -lo, 0.0)))
            k = 128 * (2 * p + e)
            da[:, k:k + 128] = dop * own_m[e] + low(tail)
    at_ = ab[...].T
    q3 = 3 * d
    hq = q3 // 2
    gwo = low(dot(at_, ga))
    gq[:, hq:hq + hd] = gwo[:, :hd]
    gq[:, 2 * hq + hd:2 * hq + 2 * hd] = gwo[:, hd:]

    plane = [((lax.rem(lax.div(dp, 2) + n, nq) * 2 + c), z) for n in range(1, nq)]
    column = [(dp, lax.rem(z + n, nb)) for n in range(1, nb)]

    def exchange(src, got, sems, first, to, start):
        for n, t in enumerate(to):
            cp = link(src, got.at[first + n], sems, first + n, t)
            cp.start() if start else cp.wait()
        if not start:
            v = src[...]
            for n in range(len(to)):
                v = v + got[first + n]
            src[...] = v

    def vec_step(n):
        mine = pl.ds(pl.multiple_of(8 * c, 8), 8)
        other = pl.ds(pl.multiple_of(8 - 8 * c, 8), 8)
        halves = link(fv.at[other], rv.at[0], vsem, 0, peer)
        back_ = link(vhalf, fv.at[mine], vsem, nq + nb - 1, peer)
        if n == 0:
            halves.start()
        elif n == 1:
            halves.wait()
            vhalf[...] = fv[mine] + rv[0]
            exchange(vhalf, rv, vsem, 1, plane, True)
        elif n == 2:
            exchange(vhalf, rv, vsem, 1, plane, False)
            exchange(vhalf, rv, vsem, nq, column, True)
        elif n == 3:
            exchange(vhalf, rv, vsem, nq, column, False)
            back_.start()
        else:
            back_.wait()
            fv[mine] = vhalf[...]

    def vec2_step(n):
        groups = [(0, [peer]), (1, plane), (nq, column)]
        if n > 0:
            exchange(vec2, rv2, vsem2, *groups[n - 1], False)
        if n < 3:
            exchange(vec2, rv2, vsem2, *groups[n], True)

    def kvcopy(p):
        src = wd.at[pl.ds(pl.multiple_of(p * 512, 16), rows), pl.ds(0, 256)]
        return pltpu.make_async_remote_copy(src_ref=src, dst_ref=kvrecv.at[p], send_sem=kvsem.at[0, p],
                                            recv_sem=kvsem.at[1, p], device_id=peer, device_id_type=MESH)

    def pair_step(p, _):
        dq = [None, None]
        for n in range(2):
            h = (1 - c) if n == 0 else c
            kp = kall[p, h]
            vp = vall[p, h]
            bias = kb[pl.ds(pl.multiple_of(h * rows, 16), rows), :]
            kt = kp.T
            dks, dvs = [], []
            for e in range(2):
                kx = kp * own_m[e] + (bias * at_aux(e, 0, 0) + at_aux(e, 1, 3))
                vx = vp * own_m[e] + at_aux(e, 0, 2)
                q = qa[2 * p + e]
                do = da[:, pl.ds(pl.multiple_of((2 * p + e) * 128, 128), 128)]
                pt = jnp.exp(dot(kx, q, NT))
                ds = low(pt * dot(vx, do, NT))
                dvs.append(dot(low(pt), do))
                dks.append(dot(ds, q))
                t = dot(kt[64 * e:64 * e + 64, :], ds)
                dq[e] = t if dq[e] is None else dq[e] + t
            dk = jnp.where(lane < 64, dks[0], dks[1])
            dv = jnp.where(lane < 64, dvs[0], dvs[1])
            if n == 0:
                at = pl.ds(pl.multiple_of(p * 512, 16), rows)
                wd[at, 0:128] = low(dk)
                wd[at, 128:256] = low(dv)
                kvcopy(p).start()
            else:
                o_s[p] = dk
                acc[:, pl.ds(pl.multiple_of(p * 128, 128), 128)] = dv
        dqp = jnp.concatenate(dq, axis=0).T * 0.125
        dqkv[:, pl.ds(pl.multiple_of(p * 128, 128), 128)] = low(dqp)
        return 0

    part_q = [(0, 2 * hd), (2 * hd, hq + hd)]
    jq = []
    for t in range(2):
        for i in range(2):
            at0 = t * (hq + hd) + i * 2 * hd
            jq.append(make(4 + 2 * t + i, ((0, 1, 2), (0, 2, 1))[i], functools.partial(
                lambda at0, p: rows_of(gq, p, at0, 2 * hd), at0)))
    half = pairs // 2

    def finish_pairs(t):
        for p in range(t * half, t * half + half):
            kvcopy(p).wait()
            dqkv[:, d + 128 * p:d + 128 * p + 128] = low(o_s[p] + kvrecv[p, :, 0:128].astype(F32))
            dqkv[:, 2 * d + 128 * p:2 * d + 128 * p + 128] = low(
                acc[:, 128 * p:128 * p + 128] + kvrecv[p, :, 128:256].astype(F32))
        xt = xm[...].reshape(rows, d).T
        for n in range(3):
            at = t * (hq + hd) + n * hd
            gq[:, at:at + hd] = low(dot(xt, dqkv[:, n * d + t * hd:n * d + t * hd + hd]))
            if n == 1:
                jq[2 * t].start()
        jq[2 * t + 1].start()

    zd = Pieces(dp, z, nbits, *zbufs[0:4], jsem[8])
    zu = Pieces(dp, z, nbits, *zbufs[4:8], jsem[9])
    zq = Pieces(dp, z, nbits, *zbufs[8:12], jsem[10])

    pr_z = d // nb

    def at_p(k, what):
        def f(p):
            @pl.when(p == k)
            def _():
                what()
        return f

    def step1():
        vec_step(1)

    def step2():
        jd[0].next2()
        jd[1].next2()
        ju[0].next1()
        ju[1].next1()

    def step3():
        finish_pairs(0)
        vec_step(2)

    def step4():
        vd = jnp.concatenate([jd[0].result(), jd[1].result()], axis=0)
        for j in range(nb):
            zd.zs[j % 2, j // 2] = low(vd[pr_z * j:pr_z * j + pr_z, :])
        zd.start()
        weights[0].start()

    def step5():
        jq[0].next1()
        jq[1].next1()
        vec_step(3)

    vec_step(0)
    todo = [at_p(1, step1), at_p(2, step2), at_p(3, step3), at_p(4, step4), at_p(5, step5)]

    def step(p, carry):
        for t in todo:
            t(p)
        return pair_step(p, carry)

    lax.fori_loop(0, pairs, step, 0)
    finish_pairs(1)
    weights[0].wait()
    for n in range(3):
        n1_s[...] += dot(dqkv[:, n * d:n * d + d], wq[:, n * d:n * d + d], NT)
    dx = low(n1_s[...])
    dxs[...] = dx.reshape(dxs.shape)
    zd.next1()
    vec_step(4)
    back(dxs, dx_z, sd, rd, True)
    third = d // 3
    for n, k in ((0, 0), (1, 2 * d)):
        t = total(dqkv[:, k:k + d].astype(F32))
        for i in range(3):
            vec2[3 * n + i:3 * n + i + 1, :] = t[:, third * i:third * i + third]
    vec2[6:8, :] = jnp.zeros((2, third), F32)
    vec2_step(0)
    ju[0].next2()
    ju[1].next2()
    jq[2].next1()
    jq[3].next1()
    vec2_step(1)
    jq[0].next2()
    jq[1].next2()
    vec2_step(2)
    vu = [ju[0].result(), ju[1].result()]
    n = ff // nb
    for j in range(nb):
        k = j * n
        zu.zs[j % 2, j // 2] = low(vu[k // hf][:, k % hf:k % hf + n])
    zu.start()
    fd[...] = zd.result()
    jq[2].next2()
    jq[3].next2()
    zu.next1()
    vec2_step(3)
    for n in range(2):
        for i in range(3):
            fv[12 + n:13 + n, third * i:third * i + third] = vec2[3 * n + i:3 * n + i + 1, :]
    va = [jq[0].result(), jq[1].result()]
    vb = [jq[2].result(), jq[3].result()]
    cols = []
    for n, (i, k) in enumerate(((0, 0), (0, 1), (1, 0), (1, 1))):
        cols += [va[i][:, k * hd:k * hd + hd], vb[i][:, k * hd:k * hd + hd]]
    v = jnp.concatenate(cols, axis=1)
    rolled = pltpu.roll(v, v.shape[1] - 64, 1)
    for j in range(nb):
        at = 0
        for first, w in ((0, q3 // nb), (q3, d // nb)):
            s0 = first + w * j
            r = s0 % 128
            wide = -(-w // 128) * 128
            zq.zs[j % 2, j // 2, :, at:at + wide] = low((rolled if r else v)[:, s0 - r:s0 - r + wide])
            at += wide
    zq.start()
    fu[...] = zu.result()
    back(om, out_z, so, ro, False)
    back_in(om, out_z, ro)
    zq.next1()
    back(dxs, dx_z, sd, rd, False)
    back_in(dxs, dx_z, rd)
    fq[...] = zq.result()


def layer(nbits, nb, lengths, speech, grad_output, vectors, w_qkv, w_out, w_up, w_down):
    blk_len, d = speech.shape[1:]
    hp = -(-blk_len // 32) * 16
    heads = d // 64
    rows = nb * hp
    pairs = d // 128
    ff = w_up.shape[1]
    pr, pf = d // 8, ff // 8
    wide = -(-(3 * d // nb) // 128) * 128 + -(-(d // nb) // 128) * 128
    extra = nbits - 3
    nq = (1 << nbits) // 2
    out = [
        jax.ShapeDtypeStruct((2, 2 * hp, d), BF16),
        jax.ShapeDtypeStruct((2, 2 * hp, d), BF16),
        jax.ShapeDtypeStruct((d // nb, pf), F32),
        jax.ShapeDtypeStruct((pr, ff // nb), F32),
        jax.ShapeDtypeStruct((pr, wide), F32),
        jax.ShapeDtypeStruct((16, d), F32),
    ]
    dma = pltpu.SemaphoreType.DMA

    def job(r, c):
        return [VMEM((2, 2, r, c), BF16), VMEM((2, r, c), BF16), VMEM((r, c), BF16)]

    def pieces(r, c):
        more = (extra, r, c) if extra else (8, 128)
        return [VMEM((2, 2, r, c), BF16), VMEM((2, r, c), BF16), VMEM((r, c), BF16), VMEM(more, BF16)]

    scratch = [
        VMEM(w_qkv.shape, BF16), VMEM(w_out.shape, BF16), VMEM(w_up.shape, BF16), VMEM(w_down.shape, BF16),
        VMEM((nb, hp, d), BF16), VMEM((nb, hp, d), BF16), VMEM((nb, hp, d), BF16),
        VMEM((heads, rows, 128), BF16), VMEM((pairs, 2, rows, 128), BF16), VMEM((pairs, 2, rows, 128), BF16),
        VMEM((2 * rows, 128), BF16), VMEM((pairs, rows, 128), F32), VMEM((rows, d), BF16),
        VMEM((rows, d), BF16), VMEM((rows, 128), F32),
        VMEM((rows, ff), BF16), VMEM((rows, ff), BF16),
        VMEM((rows, d), F32), VMEM((rows, d), F32),
        VMEM((d // 2, ff), BF16), VMEM((d, ff), BF16), VMEM((pairs, rows, 256), BF16),
        VMEM((2, 2, 8, 128), F32), VMEM((nq + nb - 1, 8, d), F32), VMEM((8, d), F32),
        VMEM((nq + nb - 1, 8, d // 3), F32), VMEM((8, d // 3), F32),
    ]
    scratch += job(d // 2, pf) * 2 + job(pr, ff // 2) * 2 + job(pr, d) * 4
    scratch += pieces(d // nb, pf) + pieces(pr, ff // nb) + pieces(pr, wide)
    scratch += [dma((4,)), dma((2,)), dma((2, pairs)), dma((2, 2)), dma((2, nq + nb)), dma((2, nq + nb - 1))]
    scratch += [dma((4,))] * 8
    scratch += [dma((2, 6))] * 8 + [dma((2, 2 + extra))] * 3
    return pl.pallas_call(
        functools.partial(layer_kernel, (nb, hp, nbits, heads)),
        name="layer",
        out_shape=out,
        in_specs=[pl.BlockSpec(memory_space=pltpu.SMEM)] + [VM] * 11 + [ANY] * 4,
        out_specs=[VM] * len(out),
        scratch_shapes=scratch,
        compiler_params=pltpu.CompilerParams(collective_id=0, has_side_effects=True, vmem_limit_bytes=64 << 20),
    )(lengths, speech, grad_output, *vectors, w_qkv, w_out, w_up, w_down)


def finish_kernel(blk_len, cols, out_z, dx_z, fd, fu, fq, fv, out, dx, gq, bq, bv, go, bo, g1, s1, gu, bu, gd, bd, g2, s2):
    wq, wo, at = cols
    d = dx.shape[2]
    out[...] = out_z[:, :blk_len]
    dx[...] = dx_z[:, :blk_len].astype(F32)
    gq[...] = fq[:, :wq]
    go[...] = fq[:, at:at + wo]
    gu[...] = fu[...]
    gd[...] = fd[...]
    for ref, n in ((g2, 0), (s2, 1), (bd, 2), (g1, 3), (s1, 4), (bo, 5), (bq, 12), (bv, 13)):
        ref[...] = fv[n:n + 1, :].reshape(d)
    for n in range(bu.shape[0] // d):
        bu[d * n:d * n + d] = fv[8 + n:9 + n, :].reshape(d)


def shards(speech, lengths, grad_output, w_qkv, bias_query, bias_value, w_out, bias_out, gain_first, shift_first,
           w_up, bias_up, w_down, bias_down, gain_second, shift_second):
    utts, blk_len, d = speech.shape
    nb = lax.axis_size("blk")
    ndp = lax.axis_size("dp")
    nbits = ndp.bit_length() - 1
    ff = bias_up.shape[0]
    vectors = (bias_query, bias_value, bias_out, gain_first, shift_first, bias_up, bias_down, gain_second, shift_second)
    got = layer(nbits, nb, lengths, speech, grad_output, vectors, w_qkv, w_out, w_up, w_down)
    wq, wo = 3 * d // nb, d // nb
    at = -(-wq // 128) * 128
    shape = jax.ShapeDtypeStruct
    vec = shape((d,), F32)
    res = pl.pallas_call(
        functools.partial(finish_kernel, blk_len, (wq, wo, at)),
        name="finish",
        out_shape=[
            shape((utts, blk_len, d), BF16), shape((utts, blk_len, d), F32), shape((d // 8, wq), F32), vec, vec,
            shape((d // 8, wo), F32), vec, vec, vec, shape((d // 8, ff // nb), F32), shape((ff,), F32),
            shape((wo, ff // 8), F32), vec, vec, vec,
        ],
        in_specs=[VM] * 6,
        out_specs=[VM] * 15,
        compiler_params=pltpu.CompilerParams(vmem_limit_bytes=60 << 20),
    )(*got)
    res = list(res)
    res[11] = res[11].T
    parts = ndp // 8
    if parts > 1:
        sub = lax.rem(lax.axis_index("dp"), parts)
        for i in (2, 5, 9, 11):
            n = res[i].shape[0] // parts
            res[i] = lax.dynamic_slice_in_dim(res[i], sub * n, n, 0)
    return tuple(res)


def solution(mesh):
    rows = P("dp", "blk", None)
    cut = P("dp", "blk")
    return jax.shard_map(
        shards,
        mesh=mesh,
        in_specs=(rows, P("dp"), rows) + (P(),) * 13,
        out_specs=(rows, rows, cut, P(), P(), cut, P(), P(), P(), cut, P(), cut, P(), P(), P()),
        check_vma=False,
    )
```

time: 582 us -> 146 us (0.25); the launches traced: 571 us -> 146 us
  waiting for transfers between devices: 176 us -> 0 us
  matrix products: 150 us -> 0 us
  Pallas kernels: 0 us -> 145 us
  local copies, waits for them, and re-layouts: 132 us -> 0 us
  other arithmetic: 53.1 us -> 0 us
  blocking collectives: 40.3 us -> 0 us
  between operations: 15.5 us -> 0.84 us
    dot_general x36 -> x0, matrix products: 150 us -> none  [the longest x4 20.8 us: shards(): jnp.einsum('uhqk,uqhd->ukhd', probabilities.astype(jnp.bfloat16), grad_he...]
    pallas_call x0 -> x2, Pallas kernels: none -> 145 us  [the longest x1 142 us: layer(): pl.pallas_call(functools.partial(layer_kernel, (nb, hp, nbits, heads)), n...]
    ppermute x7 -> x0, waiting for transfers between devices: 85.1 us -> none  [shifted(): return lax.ppermute(block, axis, route)]
    unnamed x11 -> x0, waiting for transfers between devices: 77.6 us -> none
    slice x14 -> x0, local copies, waits for them, and re-layouts: 41.3 us -> none  [the longest x5 11.7 us: shards(): moving[1]]
    psum x1 -> x0, blocking collectives: 40.3 us -> none  [shards(): lax.psum((grad_bias_query, grad_bias_value, grad_bias_out, grad_gain_firs...]
    unnamed x167 -> x0, local copies, waits for them, and re-layouts: 30 us -> none
    another operation x8 -> x0, local copies, waits for them, and re-layouts: 23.2 us -> none  [shards(): carried = carried + jnp.stack([part_keys, part_values])]
  transfers between devices with their start and end apart: 15 -> 0, of which waited for: 10 -> 0; matrix products, arithmetic and copies ran while one was open for 41% -> 0% of each run, Pallas kernels for 0% -> 0%
where the time goes in v2:
time: 146 us
  Pallas kernels  145 us (99%)
    pallas_call x1, Pallas kernels, layer(): pl.pallas_call(functools.partial(layer_kernel, (nb, hp, nbits, heads)), n...  142 us
    pallas_call x1, Pallas kernels, shards(): pl.pallas_call(functools.partial(finish_kernel, blk_len, (wq, wo, at)), n...  3.28 us

profile of v2, /device:TPU:0, one launch (start us, length us, event | category | flops | bytes accessed | tf_op | source)
XLA Modules:
  0.0 146.3 jit_solution(11703530267968968345)
XLA Ops:
  0.7 142.1 %layer.1 = (bf16[2,224,768]{2,1,0:T(8,128)(2,1)}, bf16[2,224,768]{2,1,0:T(8,128)(2,1)}, f32[192,384]{1,0:T(8,128)}, f32[96,768]{1,0:T(8,128)}, f32[96,896]{1,0:T(8,128)}, /*index=5*/f32[16,768]{1,0:T(8,128)}) custom-call(s32[2]{0:T(128)} %len_ref.1, bf16[2,216,768]{2,1,0:T(8,128)(2,1)} %x_ref.1, bf16[2,216,768]{2,1,0:T(8,128)(2,1)} %g_ref.1, f32[768]{0:T(1024)} %bq.1, ...), custom_call_target="tpu_custom_call" | custom-call | tf_op jit(solution)/shard_map/layer/pallas_call | solution.py:701
  142.8 3.3 %finish.1 = (bf16[2,216,768]{2,1,0:T(8,128)(2,1)}, f32[2,216,768]{2,1,0:T(8,128)}, f32[96,576]{1,0:T(8,128)}, f32[768]{0:T(1024)}, f32[768]{0:T(1024)}, /*index=...) custom-call(bf16[2,224,768]{2,1,0:T(8,128)(2,1)} %get-tuple-element., ...), custom_call_target="tpu_custom_call" | custom-call | tf_op jit(solution)/shard_map/finish/pallas_call | solution.py:740

commit v3 on v2

--- a/solution.py
+++ b/solution.py
@@ -160,7 +160,7 @@
     (wq, wo, wu, wd, xm, gm, om, qa, kall, vall, kb, o_s, ab, nl, inv1, act, fac, n1_s, acc, gwd, gwu, kvrecv, lens, rv, vhalf, rv2, vec2,
      *rest) = scratch
     jobs, rest = rest[:24], rest[24:]
-    zbufs, (wsem, lsem, kvsem, kvs2, vsem, vsem2, sx, rx, sg, rg, so, ro, sd, rd, *jsem) = rest[:12], rest[12:]
+    zbufs, (wsem, lsem, kvsem, kvs2, vsem, vsem2, sx, rx, sg, rg, so, ro, sd, rd, *jsem) = rest[:16], rest[16:]
     blk_len, d = x_ref.shape[1:]
     dp, z = lax.axis_index("dp"), lax.axis_index("blk")
     c = lax.rem(dp, 2)
@@ -262,20 +262,22 @@
     spread(out_z, xm, sx, rx, False)
     spread(dx_z, gm, sg, rg, True)
     x = xm[...].reshape(rows, d)
-    kvs = []
-    for part, scr in ((1, kall), (2, vall)):
-        for p in range(pairs // 2):
-            at = part * d + 256 * p
+
+    def kv_in(n, p):
+        scr = (kall, vall)[n]
+        return pltpu.make_async_remote_copy(src_ref=scr.at[p, c], dst_ref=scr.at[p, c], send_sem=kvs2.at[0, n, p],
+                                            recv_sem=kvs2.at[1, n, p], device_id=peer, device_id_type=MESH)
+
+    for p in range(pairs // 2):
+        for n, scr in enumerate((kall, vall)):
+            at = (n + 1) * d + 256 * p
             t = dot(x, wq[:, at:at + 256])
-            if part == 2:
+            if n == 1:
                 t = t + row(bv)[:, 256 * p:256 * p + 256]
             t = low(t)
             for e in range(2):
                 scr[2 * p + e, c] = t[:, 128 * e:128 * e + 128]
-        kv = pltpu.make_async_remote_copy(src_ref=scr.at[:, c], dst_ref=scr.at[:, c], send_sem=kvs2.at[0, part - 1],
-                                          recv_sem=kvs2.at[1, part - 1], device_id=peer, device_id_type=MESH)
-        kv.start()
-        kvs.append(kv)
+                kv_in(n, 2 * p + e).start()
     for p in range(pairs // 2):
         at = 256 * p
         t = low(dot(x, wq[:, at:at + 256]) + row(bq)[:, at:at + 256])
@@ -291,10 +293,10 @@
             frame = (t + blk_len * b).astype(F32)
             ok = jnp.logical_and(t < blk_len, frame < usable_len)
             kb[pl.ds((h * nb + b) * hp, hp), :] = low(jnp.where(ok, 0.0, MASKED))
-    for kv in kvs:
-        kv.wait()
 
     def attend_step(p, _):
+        for n in range(2):
+            kv_in(n, p).wait()
         kp = kall[p].reshape(2 * rows, 128)
         vp = vall[p].reshape(2 * rows, 128)
         bias = kb[...]
@@ -316,7 +318,7 @@
         o_s[p] = jnp.where(lane < 64, outs[0], outs[1])
         return 0
 
-    lax.fori_loop(0, pairs, attend_step, 0)
+    lax.fori_loop(0, pairs, attend_step, 0, unroll=2)
 
     for p in range(pairs):
         ab[:, 128 * p:128 * p + 128] = low(o_s[p])
@@ -364,7 +366,6 @@
         return 0
 
     lax.fori_loop(0, nb, norm2, 0)
-    back(om, out_z, so, ro, True)
     gb = gm[...].reshape(rows, d)
     gbt = gb.T
 
@@ -382,7 +383,7 @@
                      pl.ds(pl.multiple_of(lax.rem(p, across) * pf, 128), pf)]
 
     jd = [make(i, ((0, 1, 2), (0, 2, 1))[i], functools.partial(down_part, i)) for i in range(2)]
-    ju = [make(2 + i, ((0, 1, 2), (0, 2, 1))[i], functools.partial(
+    ju = [make(2 + i, ((0, 2, 1), (0, 1, 2))[i], functools.partial(
         lambda i, p: rows_of(gwu, p, i * hf, hf), i)) for i in range(2)]
     for i in range(2):
         for p in range(0, 8, 2):
@@ -401,11 +402,12 @@
             fv[8 + k // d:9 + k // d, k % d:k % d + 128] = bup[:, 128 * i:128 * i + 128]
         acc[...] += dot(gu, wu[:, at], NT)
         gwu[:, at] = low(dot(nt, gu))
-        if j == 1:
+        if j == 2:
+            ju[0].start()
+            jd[1].next1()
             jd[0].next1()
-        if j == 2:
-            jd[1].next1()
-            ju[0].start()
+        if j == 3:
+            back(om, out_z, so, ro, True)
     ju[1].start()
 
     def norm1_back(i, _):
@@ -545,7 +547,7 @@
 
     zd = Pieces(dp, z, nbits, *zbufs[0:4], jsem[8])
     zu = Pieces(dp, z, nbits, *zbufs[4:8], jsem[9])
-    zq = Pieces(dp, z, nbits, *zbufs[8:12], jsem[10])
+    zq = [Pieces(dp, z, nbits, *zbufs[8 + 4 * i:12 + 4 * i], jsem[10 + i]) for i in range(2)]
 
     pr_z = d // nb
 
@@ -556,29 +558,36 @@
                 what()
         return f
 
-    def step1():
-        vec_step(1)
-
-    def step2():
-        jd[0].next2()
-        jd[1].next2()
-        ju[0].next1()
-        ju[1].next1()
-
-    def step3():
-        finish_pairs(0)
-        vec_step(2)
-
-    def step4():
+    def start_down():
         vd = jnp.concatenate([jd[0].result(), jd[1].result()], axis=0)
         for j in range(nb):
             zd.zs[j % 2, j // 2] = low(vd[pr_z * j:pr_z * j + pr_z, :])
         zd.start()
+
+    def start_up():
+        vu = [ju[0].result(), ju[1].result()]
+        n = ff // nb
+        for j in range(nb):
+            k = j * n
+            zu.zs[j % 2, j // 2] = low(vu[k // hf][:, k % hf:k % hf + n])
+        zu.start()
+
+    def step1():
+        vec_step(1)
+        ju[1].next1()
+
+    def step2():
+        ju[0].next1()
+
+    def step3():
+        vec_step(2)
+
+    def step4():
         weights[0].start()
 
     def step5():
-        jq[0].next1()
-        jq[1].next1()
+        finish_pairs(0)
+        jd[1].next2()
         vec_step(3)
 
     vec_step(0)
@@ -590,14 +599,13 @@
         return pair_step(p, carry)
 
     lax.fori_loop(0, pairs, step, 0)
+    jd[0].next2()
     finish_pairs(1)
+    vec_step(4)
     weights[0].wait()
     for n in range(3):
         n1_s[...] += dot(dqkv[:, n * d:n * d + d], wq[:, n * d:n * d + d], NT)
-    dx = low(n1_s[...])
-    dxs[...] = dx.reshape(dxs.shape)
-    zd.next1()
-    vec_step(4)
+    dxs[...] = low(n1_s[...]).reshape(dxs.shape)
     back(dxs, dx_z, sd, rd, True)
     third = d // 3
     for n, k in ((0, 0), (1, 2 * d)):
@@ -606,51 +614,56 @@
             vec2[3 * n + i:3 * n + i + 1, :] = t[:, third * i:third * i + third]
     vec2[6:8, :] = jnp.zeros((2, third), F32)
     vec2_step(0)
+    ju[1].next2()
     ju[0].next2()
-    ju[1].next2()
+    start_down()
+    jq[3].next1()
     jq[2].next1()
-    jq[3].next1()
     vec2_step(1)
+    start_up()
+    jq[1].next1()
+    jq[0].next1()
+    jq[3].next2()
+    vec2_step(2)
+    zd.next1()
+    jq[2].next2()
     jq[0].next2()
     jq[1].next2()
-    vec2_step(2)
-    vu = [ju[0].result(), ju[1].result()]
-    n = ff // nb
+    zu.next1()
+    va = [jq[0].result(), jq[1].result()]
+    vb = [jq[2].result(), jq[3].result()]
+    cols = []
+    for i, k in ((0, 0), (0, 1), (1, 0), (1, 1)):
+        cols += [va[i][:, k * hd:k * hd + hd], vb[i][:, k * hd:k * hd + hd]]
+    v = jnp.concatenate(cols, axis=1)
+    left = pltpu.roll(v, v.shape[1] - 64, 1)
+    right = pltpu.roll(v, 64, 1)
+    wide = q3 // nb
+    cut = wide - 64
+    lane_p = lane_of((pr, 128))
     for j in range(nb):
-        k = j * n
-        zu.zs[j % 2, j // 2] = low(vu[k // hf][:, k % hf:k % hf + n])
-    zu.start()
-    fd[...] = zd.result()
-    jq[2].next2()
-    jq[3].next2()
-    zu.next1()
+        s0, s1_ = wide * j, q3 + d // nb * j
+        a = v[:, s0:s0 + wide + 64] if j % 2 == 0 else left[:, s0 - 64:s0 + wide]
+        b = right[:, s1_:s1_ + 256] if j % 2 == 0 else v[:, s1_ - 64:s1_ + 192]
+        piece = low(jnp.concatenate([a[:, :cut], jnp.where(lane_p < 64, a[:, cut:], b[:, :128]), b[:, 128:]], axis=1))
+        for i in range(2):
+            zq[i].zs[j % 2, j // 2] = piece[pr // 2 * i:pr // 2 * i + pr // 2]
+    zq[0].start()
+    zq[1].start()
     vec2_step(3)
     for n in range(2):
         for i in range(3):
             fv[12 + n:13 + n, third * i:third * i + third] = vec2[3 * n + i:3 * n + i + 1, :]
-    va = [jq[0].result(), jq[1].result()]
-    vb = [jq[2].result(), jq[3].result()]
-    cols = []
-    for n, (i, k) in enumerate(((0, 0), (0, 1), (1, 0), (1, 1))):
-        cols += [va[i][:, k * hd:k * hd + hd], vb[i][:, k * hd:k * hd + hd]]
-    v = jnp.concatenate(cols, axis=1)
-    rolled = pltpu.roll(v, v.shape[1] - 64, 1)
-    for j in range(nb):
-        at = 0
-        for first, w in ((0, q3 // nb), (q3, d // nb)):
-            s0 = first + w * j
-            r = s0 % 128
-            wide = -(-w // 128) * 128
-            zq.zs[j % 2, j // 2, :, at:at + wide] = low((rolled if r else v)[:, s0 - r:s0 - r + wide])
-            at += wide
-    zq.start()
+    fd[...] = zd.result()
+    zq[0].next1()
     fu[...] = zu.result()
+    zq[1].next1()
     back(om, out_z, so, ro, False)
     back_in(om, out_z, ro)
-    zq.next1()
     back(dxs, dx_z, sd, rd, False)
     back_in(dxs, dx_z, rd)
-    fq[...] = zq.result()
+    for i in range(2):
+        fq[pr // 2 * i:pr // 2 * i + pr // 2, :] = zq[i].result()
 
 
 def layer(nbits, nb, lengths, speech, grad_output, vectors, w_qkv, w_out, w_up, w_down):
@@ -661,7 +674,7 @@
     pairs = d // 128
     ff = w_up.shape[1]
     pr, pf = d // 8, ff // 8
-    wide = -(-(3 * d // nb) // 128) * 128 + -(-(d // nb) // 128) * 128
+    wide = 4 * d // nb
     extra = nbits - 3
     nq = (1 << nbits) // 2
     out = [
@@ -694,10 +707,10 @@
         VMEM((nq + nb - 1, 8, d // 3), F32), VMEM((8, d // 3), F32),
     ]
     scratch += job(d // 2, pf) * 2 + job(pr, ff // 2) * 2 + job(pr, d) * 4
-    scratch += pieces(d // nb, pf) + pieces(pr, ff // nb) + pieces(pr, wide)
-    scratch += [dma((4,)), dma((2,)), dma((2, pairs)), dma((2, 2)), dma((2, nq + nb)), dma((2, nq + nb - 1))]
+    scratch += pieces(d // nb, pf) + pieces(pr, ff // nb) + pieces(pr // 2, wide) * 2
+    scratch += [dma((4,)), dma((2,)), dma((2, pairs)), dma((2, 2, pairs)), dma((2, nq + nb)), dma((2, nq + nb - 1))]
     scratch += [dma((4,))] * 8
-    scratch += [dma((2, 6))] * 8 + [dma((2, 2 + extra))] * 3
+    scratch += [dma((2, 6))] * 8 + [dma((2, 2 + extra))] * 4
     return pl.pallas_call(
         functools.partial(layer_kernel, (nb, hp, nbits, heads)),
         name="layer",
@@ -710,12 +723,12 @@
 
 
 def finish_kernel(blk_len, cols, out_z, dx_z, fd, fu, fq, fv, out, dx, gq, bq, bv, go, bo, g1, s1, gu, bu, gd, bd, g2, s2):
-    wq, wo, at = cols
+    wq, wo = cols
     d = dx.shape[2]
     out[...] = out_z[:, :blk_len]
     dx[...] = dx_z[:, :blk_len].astype(F32)
     gq[...] = fq[:, :wq]
-    go[...] = fq[:, at:at + wo]
+    go[...] = pltpu.roll(fq[:, wq - 64:], 192, 1)[:, :wo]
     gu[...] = fu[...]
     gd[...] = fd[...]
     for ref, n in ((g2, 0), (s2, 1), (bd, 2), (g1, 3), (s1, 4), (bo, 5), (bq, 12), (bv, 13)):
@@ -734,11 +747,10 @@
     vectors = (bias_query, bias_value, bias_out, gain_first, shift_first, bias_up, bias_down, gain_second, shift_second)
     got = layer(nbits, nb, lengths, speech, grad_output, vectors, w_qkv, w_out, w_up, w_down)
     wq, wo = 3 * d // nb, d // nb
-    at = -(-wq // 128) * 128
     shape = jax.ShapeDtypeStruct
     vec = shape((d,), F32)
     res = pl.pallas_call(
-        functools.partial(finish_kernel, blk_len, (wq, wo, at)),
+        functools.partial(finish_kernel, blk_len, (wq, wo)),
         name="finish",
         out_shape=[
             shape((utts, blk_len, d), BF16), shape((utts, blk_len, d), F32), shape((d // 8, wq), F32), vec, vec,

time: 146 us -> 139 us (0.952)
  Pallas kernels: 145 us -> 138 us
    pallas_call x1, Pallas kernels: 142 us -> 135 us  [layer(): pl.pallas_call(functools.partial(layer_kernel, (nb, hp, nbits, heads)), n...]
where the time goes in v3:
time: 139 us
  Pallas kernels  138 us (99%)
    pallas_call x1, Pallas kernels, layer(): pl.pallas_call(functools.partial(layer_kernel, (nb, hp, nbits, heads)), n...  135 us
    pallas_call x1, Pallas kernels, shards(): pl.pallas_call(functools.partial(finish_kernel, blk_len, (wq, wo)), name=...  3.28 us

profile of v3, /device:TPU:0, one launch (start us, length us, event | category | flops | bytes accessed | tf_op | source)
XLA Modules:
  0.0 139.2 jit_solution(3928020794248252914)
XLA Ops:
  0.7 135.0 %layer.1 = (bf16[2,224,768]{2,1,0:T(8,128)(2,1)}, bf16[2,224,768]{2,1,0:T(8,128)(2,1)}, f32[192,384]{1,0:T(8,128)}, f32[96,768]{1,0:T(8,128)}, f32[96,768]{1,0:T(8,128)}, /*index=5*/f32[16,768]{1,0:T(8,128)}) custom-call(s32[2]{0:T(128)} %len_ref.1, bf16[2,216,768]{2,1,0:T(8,128)(2,1)} %x_ref.1, bf16[2,216,768]{2,1,0:T(8,128)(2,1)} %g_ref.1, f32[768]{0:T(1024)} %bq.1, ...), custom_call_target="tpu_custom_call" | custom-call | tf_op jit(solution)/shard_map/layer/pallas_call | solution.py:714
  135.7 3.3 %finish.1 = (bf16[2,216,768]{2,1,0:T(8,128)(2,1)}, f32[2,216,768]{2,1,0:T(8,128)}, f32[96,576]{1,0:T(8,128)}, f32[768]{0:T(1024)}, f32[768]{0:T(1024)}, /*index=...) custom-call(bf16[2,224,768]{2,1,0:T(8,128)(2,1)} %get-tuple-element., ...), custom_call_target="tpu_custom_call" | custom-call | tf_op jit(solution)/shard_map/finish/pallas_call | solution.py:752

commit v4 on v3

--- a/solution.py
+++ b/solution.py
@@ -155,7 +155,7 @@
 
 
 def layer_kernel(geo, len_ref, x_ref, g_ref, bq, bv, bo, g1, s1, bu, bd, g2, s2, wq_hbm, wo_hbm, wu_hbm, wd_hbm,
-                 out_z, dx_z, fd, fu, fq, fv, *scratch):
+                 out_hbm, dx_hbm, fd, fu, fq, fv, out_z, dx_z, osem, *scratch):
     nb, hp, nbits, heads = geo
     (wq, wo, wu, wd, xm, gm, om, qa, kall, vall, kb, o_s, ab, nl, inv1, act, fac, n1_s, acc, gwd, gwu, kvrecv, lens, rv, vhalf, rv2, vec2,
      *rest) = scratch
@@ -185,10 +185,12 @@
     for to in greet:
         pl.semaphore_signal(barrier, inc=1, device_id=to, device_id_type=MESH)
 
-    for src, dst in ((x_ref, out_z), (g_ref, dx_z)):
+    def fill(src, dst):
         for s in range(2):
             dst[s, 2 * hp - 16:, :] = jnp.zeros((16, d), BF16)
             dst[s, 0:blk_len, :] = src[s]
+
+    fill(x_ref, out_z)
     for s in range(2):
         lens[c, s] = jnp.full((8, 128), len_ref[s], jnp.int32).astype(F32)
     pl.semaphore_wait(barrier, len(greet))
@@ -255,6 +257,7 @@
 
     spread(out_z, xm, sx, rx, True)
     lcopy.start()
+    fill(g_ref, dx_z)
     weights[0].wait()
     for w in weights[1:]:
         w.start()
@@ -575,9 +578,10 @@
     def step1():
         vec_step(1)
         ju[1].next1()
+        ju[0].next1()
 
     def step2():
-        ju[0].next1()
+        pass
 
     def step3():
         vec_step(2)
@@ -660,10 +664,15 @@
     zq[1].next1()
     back(om, out_z, so, ro, False)
     back_in(om, out_z, ro)
+    outs = [pltpu.make_async_copy(a, b, osem.at[n]) for n, (a, b) in enumerate(((out_z, out_hbm), (dx_z, dx_hbm)))]
+    outs[0].start()
     back(dxs, dx_z, sd, rd, False)
     back_in(dxs, dx_z, rd)
+    outs[1].start()
     for i in range(2):
         fq[pr // 2 * i:pr // 2 * i + pr // 2, :] = zq[i].result()
+    for o in outs:
+        o.wait()
 
 
 def layer(nbits, nb, lengths, speech, grad_output, vectors, w_qkv, w_out, w_up, w_down):
@@ -695,6 +704,7 @@
         return [VMEM((2, 2, r, c), BF16), VMEM((2, r, c), BF16), VMEM((r, c), BF16), VMEM(more, BF16)]
 
     scratch = [
+        VMEM((2, 2 * hp, d), BF16), VMEM((2, 2 * hp, d), BF16), dma((2,)),
         VMEM(w_qkv.shape, BF16), VMEM(w_out.shape, BF16), VMEM(w_up.shape, BF16), VMEM(w_down.shape, BF16),
         VMEM((nb, hp, d), BF16), VMEM((nb, hp, d), BF16), VMEM((nb, hp, d), BF16),
         VMEM((heads, rows, 128), BF16), VMEM((pairs, 2, rows, 128), BF16), VMEM((pairs, 2, rows, 128), BF16),
@@ -716,7 +726,7 @@
         name="layer",
         out_shape=out,
         in_specs=[pl.BlockSpec(memory_space=pltpu.SMEM)] + [VM] * 11 + [ANY] * 4,
-        out_specs=[VM] * len(out),
+        out_specs=[ANY] * 2 + [VM] * (len(out) - 2),
         scratch_shapes=scratch,
         compiler_params=pltpu.CompilerParams(collective_id=0, has_side_effects=True, vmem_limit_bytes=64 << 20),
     )(lengths, speech, grad_output, *vectors, w_qkv, w_out, w_up, w_down)
@@ -727,6 +737,13 @@
     d = dx.shape[2]
     out[...] = out_z[:, :blk_len]
     dx[...] = dx_z[:, :blk_len].astype(F32)
+
+    @pl.when(pl.program_id(0) == 0)
+    def _():
+        small(fd, fu, fq, fv, wq, wo, d, gq, bq, bv, go, bo, g1, s1, gu, bu, gd, bd, g2, s2)
+
+
+def small(fd, fu, fq, fv, wq, wo, d, gq, bq, bv, go, bo, g1, s1, gu, bu, gd, bd, g2, s2):
     gq[...] = fq[:, :wq]
     go[...] = pltpu.roll(fq[:, wq - 64:], 192, 1)[:, :wo]
     gu[...] = fu[...]
@@ -749,16 +766,25 @@
     wq, wo = 3 * d // nb, d // nb
     shape = jax.ShapeDtypeStruct
     vec = shape((d,), F32)
+    shapes = [
+        shape((utts, blk_len, d), BF16), shape((utts, blk_len, d), F32), shape((d // 8, wq), F32), vec, vec,
+        shape((d // 8, wo), F32), vec, vec, vec, shape((d // 8, ff // nb), F32), shape((ff,), F32),
+        shape((wo, ff // 8), F32), vec, vec, vec,
+    ]
+
+    def one(s):
+        return pl.BlockSpec((1,) + s[1:], lambda i: (i, 0, 0))
+
+    def all_of(s):
+        return pl.BlockSpec(s, lambda i: (0,) * len(s))
+
     res = pl.pallas_call(
         functools.partial(finish_kernel, blk_len, (wq, wo)),
         name="finish",
-        out_shape=[
-            shape((utts, blk_len, d), BF16), shape((utts, blk_len, d), F32), shape((d // 8, wq), F32), vec, vec,
-            shape((d // 8, wo), F32), vec, vec, vec, shape((d // 8, ff // nb), F32), shape((ff,), F32),
-            shape((wo, ff // 8), F32), vec, vec, vec,
-        ],
-        in_specs=[VM] * 6,
-        out_specs=[VM] * 15,
+        out_shape=shapes,
+        grid=(utts,),
+        in_specs=[one(got[0].shape), one(got[1].shape)] + [all_of(a.shape) for a in got[2:]],
+        out_specs=[one(a.shape) if len(a.shape) == 3 else all_of(a.shape) for a in shapes],
         compiler_params=pltpu.CompilerParams(vmem_limit_bytes=60 << 20),
     )(*got)
     res = list(res)

time: 139 us -> 139 us (level)
  no operation moved by 1% of the time
where the time goes in v4:
time: 139 us
  Pallas kernels  138 us (99%)
    pallas_call x1, Pallas kernels, layer(): pl.pallas_call(functools.partial(layer_kernel, (nb, hp, nbits, heads)), n...  135 us
    pallas_call x1, Pallas kernels, shards(): pl.pallas_call(functools.partial(finish_kernel, blk_len, (wq, wo)), name=...  3.19 us

profile of v4, /device:TPU:0, one launch (start us, length us, event | category | flops | bytes accessed | tf_op | source)
XLA Modules:
  0.0 138.7 jit_solution(4167418572811415948)
XLA Ops:
  0.7 134.6 %layer.1 = (bf16[2,224,768]{2,1,0:T(8,128)(2,1)}, bf16[2,224,768]{2,1,0:T(8,128)(2,1)}, f32[192,384]{1,0:T(8,128)}, f32[96,768]{1,0:T(8,128)}, f32[96,768]{1,0:T(8,128)}, /*index=5*/f32[16,768]{1,0:T(8,128)}) custom-call(s32[2]{0:T(128)} %len_ref.1, bf16[2,216,768]{2,1,0:T(8,128)(2,1)} %x_ref.1, bf16[2,216,768]{2,1,0:T(8,128)(2,1)} %g_ref.1, f32[768]{0:T(1024)} %bq.1, ...), custom_call_target="tpu_custom_call" | custom-call | tf_op jit(solution)/shard_map/layer/pallas_call | solution.py:724
  135.3 3.2 %finish.1 = (bf16[2,216,768]{2,1,0:T(8,128)(2,1)}, f32[2,216,768]{2,1,0:T(8,128)}, f32[96,576]{1,0:T(8,128)}, f32[768]{0:T(1024)}, f32[768]{0:T(1024)}, /*index=...) custom-call(bf16[2,224,768]{2,1,0:T(8,128)(2,1)} %get-tuple-element., ...), custom_call_target="tpu_custom_call" | custom-call | tf_op jit(solution)/shard_map/finish/pallas_call | solution.py:781
